TPU v7x, 32 devices: a whole 2x2x4 slice. The times are simulated.
32 devices in a mesh: dp: 8 (over y, x, core), seq: 4 (over z).
Axes of the slice: x: 2, y: 2, z: 4, core: 2. Of those that a mesh axis runs over, the one named last changes fastest.
Arguments:
- tokens: bfloat16 [2, 16, 608, 1024], P(None, 'dp', 'seq'), may hold values from -6 to 6
- pad_mask: int32 [2, 16, 608], P(None, 'dp', 'seq'), may hold values from 0 to 1, as said below
- image_counts: int32 [2, 8], P(None, 'dp'), may hold values from 1 to 2, as said below
- cotangent: bfloat16 [2, 16, 608, 1024], P(None, 'dp', 'seq'), may hold values from -6 to 6
- gain_one: bfloat16 [1024], P(('dp', 'seq')), may hold values from 0.099609375 to 1.8984375
- shift_one: bfloat16 [1024], P(('dp', 'seq')), may hold values from -3 to 3
- qkv_weight: bfloat16 [1024, 3072], P(('dp', 'seq')), may hold values from -0.1875 to 0.1875
- query_bias: bfloat16 [1024], P(('dp', 'seq')), may hold values from -3 to 3
- value_bias: bfloat16 [1024], P(('dp', 'seq')), may hold values from -6 to 6
- out_weight: bfloat16 [1024, 1024], P(('dp', 'seq')), may hold values from -1 to 1
- out_bias: bfloat16 [1024], P(('dp', 'seq')), may hold values from -3 to 3
- gain_two: bfloat16 [1024], P(('dp', 'seq')), may hold values from 0.099609375 to 1.8984375
- shift_two: bfloat16 [1024], P(('dp', 'seq')), may hold values from -3 to 3
- up_weight: bfloat16 [1024, 4096], P(('dp', 'seq')), may hold values from -0.1875 to 0.1875
- up_bias: bfloat16 [4096], P(('dp', 'seq')), may hold values from -3 to 3
- down_weight: bfloat16 [4096, 1024], P(('dp', 'seq')), may hold values from -0.09375 to 0.09375
- down_bias: bfloat16 [1024], P(('dp', 'seq')), may hold values from -3 to 3
Outputs:
- block_out: bfloat16 [2, 16, 608, 1024], P(None, 'dp', 'seq')
- grad_tokens: float32 [2, 16, 608, 1024], P(None, 'dp', 'seq')
- grad_gain_one: float32 [1024], P(('dp', 'seq'))
- grad_shift_one: float32 [1024], P(('dp', 'seq'))
- grad_qkv_weight: float32 [1024, 3072], P(('dp', 'seq'))
- grad_query_bias: float32 [1024], P(('dp', 'seq'))
- grad_value_bias: float32 [1024], P(('dp', 'seq'))
- grad_out_weight: float32 [1024, 1024], P(('dp', 'seq'))
- grad_out_bias: float32 [1024], P(('dp', 'seq'))
- grad_gain_two: float32 [1024], P(('dp', 'seq'))
- grad_shift_two: float32 [1024], P(('dp', 'seq'))
- grad_up_weight: float32 [1024, 4096], P(('dp', 'seq'))
- grad_up_bias: float32 [4096], P(('dp', 'seq'))
- grad_down_weight: float32 [4096, 1024], P(('dp', 'seq'))
- grad_down_bias: float32 [1024], P(('dp', 'seq'))
Inputs may be any that keep to these rules, and one draw needn't show every extreme that they name: `pad_mask`: each image's mask is 1 on its first tokens and 0 after them; more than 456 tokens of every image are 1, at most min(577, 608), and some image has exactly that many. `image_counts`: some entry is 2 and some entry is 1.
All inputs are finite; a program needn't handle non-finite values.
Results may differ from a plain program's by a relative error of at most 0.012.
Values may be sent and summed in bfloat16 or wider, within the bound.
A program may use at most 256 MiB of HBM per device.

v0:
```python
import jax
import jax.numpy as jnp
from jax import lax
from jax.sharding import PartitionSpec as P

HEADS = 16


EPSILON = 1e-06
MASKED = -1e30


def norm_rows(values, gain_vec, shift_vec):
    center = values - jnp.mean(values, -1, keepdims=True)
    spread = jnp.mean(center * center, -1, keepdims=True)
    return center * lax.rsqrt(spread + EPSILON) * gain_vec + shift_vec


def gelu_exact(values):
    return jax.nn.gelu(values, approximate=False)


def matmul(left_side, right_side):
    return jnp.dot(left_side, right_side, preferred_element_type=jnp.float32)


def matmul_tn(left_side, right_side):
    return lax.dot_general(
        left_side, right_side, (((0,), (0,)), ((), ())), preferred_element_type=jnp.float32
    )


def matmul_nt(left_side, right_side):
    return lax.dot_general(
        left_side, right_side, (((1,), (1,)), ((), ())), preferred_element_type=jnp.float32
    )


def unpack(gathered):
    return [member.astype(jnp.float32) if member.ndim == 1 else member for member in gathered]


def fetch_weights(shards):
    return unpack(
        (
            lax.all_gather(shards[0], ("dp", "seq"), axis=0, tiled=True),
            lax.all_gather(shards[1], ("dp", "seq"), axis=0, tiled=True),
            lax.all_gather(shards[2], ("dp", "seq"), axis=0, tiled=True),
            lax.all_gather(shards[3], ("dp", "seq"), axis=0, tiled=True),
            lax.all_gather(shards[4], ("dp", "seq"), axis=0, tiled=True),
            lax.all_gather(shards[5], ("dp", "seq"), axis=0, tiled=True),
            lax.all_gather(shards[6], ("dp", "seq"), axis=0, tiled=True),
            lax.all_gather(shards[7], ("dp", "seq"), axis=0, tiled=True),
            lax.all_gather(shards[8], ("dp", "seq"), axis=0, tiled=True),
            lax.all_gather(shards[9], ("dp", "seq"), axis=0, tiled=True),
            lax.all_gather(shards[10], ("dp", "seq"), axis=0, tiled=True),
            lax.all_gather(shards[11], ("dp", "seq"), axis=0, tiled=True),
            lax.all_gather(shards[12], ("dp", "seq"), axis=0, tiled=True),
        )
    )


def attend_scores(query_heads, key_heads, okay_all):
    scores = jnp.einsum(
        "sqhd,skhd->shqk", query_heads, key_heads, preferred_element_type=jnp.float32
    )
    return jnp.where(okay_all[:, None, None, :] > 0, scores, MASKED)


def on_device(
    tokens,
    pad_mask,
    image_counts,
    cotangent,
    gain_one,
    shift_one,
    qkv_weight,
    query_bias,
    value_bias,
    out_weight,
    out_bias,
    gain_two,
    shift_two,
    up_weight,
    up_bias,
    down_weight,
    down_bias,
):
    shards = (
        gain_one,
        shift_one,
        qkv_weight,
        query_bias,
        value_bias,
        out_weight,
        out_bias,
        gain_two,
        shift_two,
        up_weight,
        up_bias,
        down_weight,
        down_bias,
    )
    micro_count, slot_count, local_len, model_width = tokens.shape
    row_count = slot_count * local_len
    head_size = model_width // HEADS
    query_scale = head_size ** (-0.5)
    group_size = lax.axis_size(("dp", "seq"))
    grad_sums = [
        jnp.zeros((member.shape[0] * group_size,) + member.shape[1:], jnp.float32)
        for member in shards
    ]
    outputs = []
    input_grads = []
    for mb_index in range(micro_count):
        weight_set = fetch_weights(shards)
        (
            norm_gain,
            norm_shift,
            mix_full,
            qbias_full,
            vbias_full,
            proj_full,
            pbias_full,
            ffn_gain,
            ffn_shift,
            up_full,
            ubias_full,
            down_full,
            dbias_full,
        ) = weight_set
        input_rows = tokens[mb_index].reshape(row_count, model_width).astype(jnp.float32)
        normed_one = norm_rows(input_rows, norm_gain, norm_shift).astype(jnp.bfloat16)
        qkv_mixed = matmul(normed_one, mix_full)
        queries = ((qkv_mixed[:, :model_width] + qbias_full) * query_scale).astype(jnp.bfloat16)
        key_rows = (
            qkv_mixed[:, model_width : 2 * model_width]
            .astype(jnp.bfloat16)
            .reshape(slot_count, local_len, model_width)
        )
        value_rows = (
            (qkv_mixed[:, 2 * model_width :] + vbias_full)
            .astype(jnp.bfloat16)
            .reshape(slot_count, local_len, model_width)
        )
        key_okay = pad_mask[mb_index].astype(jnp.bfloat16)
        keys_all, values_all, okay_all = (
            lax.all_gather(key_rows, "seq", axis=1, tiled=True),
            lax.all_gather(value_rows, "seq", axis=1, tiled=True),
            lax.all_gather(key_okay, "seq", axis=1, tiled=True),
        )
        query_heads = queries.reshape(slot_count, local_len, HEADS, head_size)
        key_heads = keys_all.reshape(slot_count, -1, HEADS, head_size)
        value_heads = values_all.reshape(slot_count, -1, HEADS, head_size)
        scores = attend_scores(query_heads, key_heads, okay_all)
        row_top = jnp.max(scores, -1, keepdims=True)
        exp_scores = jnp.exp(scores - row_top)
        row_total = jnp.sum(exp_scores, -1, keepdims=True)
        attn_probs = (exp_scores / row_total).astype(jnp.bfloat16)
        log_total = row_top + jnp.log(row_total)
        attended = jnp.einsum(
            "shqk,skhd->sqhd", attn_probs, value_heads, preferred_element_type=jnp.float32
        )
        attended = attended.reshape(row_count, model_width).astype(jnp.bfloat16)
        middle = input_rows + (matmul(attended, proj_full) + pbias_full)
        normed_two = norm_rows(middle, ffn_gain, ffn_shift).astype(jnp.bfloat16)
        pre_act = matmul(normed_two, up_full) + ubias_full
        hidden = gelu_exact(pre_act).astype(jnp.bfloat16)
        result = middle + (matmul(hidden, down_full) + dbias_full)
        outputs.append(result.astype(jnp.bfloat16).reshape(slot_count, local_len, model_width))
        gathered = (
            lax.all_gather(shards[0], ("dp", "seq"), axis=0, tiled=True),
            lax.all_gather(shards[1], ("dp", "seq"), axis=0, tiled=True),
            lax.all_gather(shards[2], ("dp", "seq"), axis=0, tiled=True),
            lax.all_gather(shards[3], ("dp", "seq"), axis=0, tiled=True),
            lax.all_gather(shards[4], ("dp", "seq"), axis=0, tiled=True),
            lax.all_gather(shards[5], ("dp", "seq"), axis=0, tiled=True),
            lax.all_gather(shards[6], ("dp", "seq"), axis=0, tiled=True),
            lax.all_gather(shards[7], ("dp", "seq"), axis=0, tiled=True),
            lax.all_gather(shards[8], ("dp", "seq"), axis=0, tiled=True),
            lax.all_gather(shards[9], ("dp", "seq"), axis=0, tiled=True),
            lax.all_gather(shards[10], ("dp", "seq"), axis=0, tiled=True),
            lax.all_gather(shards[11], ("dp", "seq"), axis=0, tiled=True),
            lax.all_gather(shards[12], ("dp", "seq"), axis=0, tiled=True),
        )
        (
            norm_gain,
            norm_shift,
            mix_full,
            qbias_full,
            vbias_full,
            proj_full,
            pbias_full,
            ffn_gain,
            ffn_shift,
            up_full,
            ubias_full,
            down_full,
            dbias_full,
        ) = unpack(gathered)
        keys_all, values_all, okay_all = (
            lax.all_gather(key_rows, "seq", axis=1, tiled=True),
            lax.all_gather(value_rows, "seq", axis=1, tiled=True),
            lax.all_gather(key_okay, "seq", axis=1, tiled=True),
        )
        key_heads = keys_all.reshape(slot_count, -1, HEADS, head_size)
        value_heads = values_all.reshape(slot_count, -1, HEADS, head_size)
        slot_live = (jnp.arange(slot_count) < image_counts[mb_index, 0]).astype(jnp.float32)
        live_rows = pad_mask[mb_index].astype(jnp.float32) * slot_live[:, None]
        grad_out = (cotangent[mb_index].astype(jnp.float32) * live_rows[..., None]).reshape(
            row_count, model_width
        )
        grad_branch = grad_out.astype(jnp.bfloat16)
        d_down = matmul_tn(hidden, grad_branch)
        d_dbias = jnp.sum(grad_out, 0)
        grad_hidden = matmul_nt(grad_branch, down_full)
        gelu_back = jax.vjp(gelu_exact, pre_act)[1]
        grad_pre = gelu_back(grad_hidden)[0].astype(jnp.bfloat16)
        d_up = matmul_tn(normed_two, grad_pre)
        d_ubias = jnp.sum(grad_pre.astype(jnp.float32), 0)
        grad_normed_two = matmul_nt(grad_pre, up_full)
        second_back = jax.vjp(norm_rows, middle, ffn_gain, ffn_shift)[1]
        grad_middle, d_ffn_gain, d_ffn_shift = second_back(grad_normed_two)
        grad_middle = grad_middle + grad_out
        grad_attn = grad_middle.astype(jnp.bfloat16)
        d_proj = matmul_tn(attended, grad_attn)
        d_pbias = jnp.sum(grad_middle.astype(jnp.bfloat16).astype(jnp.float32), 0)
        grad_attended = matmul_nt(grad_attn, proj_full).astype(jnp.bfloat16)
        grad_heads = grad_attended.reshape(slot_count, local_len, HEADS, head_size)
        scores = attend_scores(query_heads, key_heads, okay_all)
        prob_exact = jnp.exp(scores - log_total)
        grad_probs = jnp.einsum(
            "sqhd,skhd->shqk", grad_heads, value_heads, preferred_element_type=jnp.float32
        )
        row_inner = jnp.sum(prob_exact * grad_probs, -1, keepdims=True)
        grad_scores = (prob_exact * (grad_probs - row_inner)).astype(jnp.bfloat16)
        grad_query = jnp.einsum(
            "shqk,skhd->sqhd", grad_scores, key_heads, preferred_element_type=jnp.float32
        )
        grad_query = (grad_query.astype(jnp.bfloat16) * query_scale).reshape(row_count, model_width)
        grad_keys_all = jnp.einsum(
            "shqk,sqhd->skhd", grad_scores, query_heads, preferred_element_type=jnp.float32
        )
        grad_values_all = jnp.einsum(
            "shqk,sqhd->skhd", attn_probs, grad_heads, preferred_element_type=jnp.float32
        )
        key_grads, value_grads = (
            lax.psum_scatter(
                grad_keys_all.reshape(slot_count, -1, model_width).astype(jnp.bfloat16),
                "seq",
                scatter_dimension=1,
                tiled=True,
            ).astype(jnp.float32),
            lax.psum_scatter(
                grad_values_all.reshape(slot_count, -1, model_width).astype(jnp.bfloat16),
                "seq",
                scatter_dimension=1,
                tiled=True,
            ).astype(jnp.float32),
        )
        key_grads = key_grads.reshape(row_count, model_width).astype(jnp.bfloat16)
        value_grads = value_grads.reshape(row_count, model_width).astype(jnp.bfloat16)
        grad_mixed = jnp.concatenate([grad_query, key_grads, value_grads], 1)
        d_mix = matmul_tn(normed_one, grad_mixed)
        d_qbias = jnp.sum(grad_query.astype(jnp.float32), 0)
        d_vbias = jnp.sum(value_grads.astype(jnp.float32), 0)
        grad_normed_one = matmul_nt(grad_mixed, mix_full)
        first_back = jax.vjp(norm_rows, input_rows, norm_gain, norm_shift)[1]
        grad_input, d_norm_gain, d_norm_shift = first_back(grad_normed_one)
        grad_input = grad_input + grad_middle
        input_grads.append(grad_input.reshape(slot_count, local_len, model_width))
        added = (
            d_norm_gain,
            d_norm_shift,
            d_mix,
            d_qbias,
            d_vbias,
            d_proj,
            d_pbias,
            d_ffn_gain,
            d_ffn_shift,
            d_up,
            d_ubias,
            d_down,
            d_dbias,
        )
        grad_sums = [total + extra for total, extra in zip(grad_sums, added)]
    owned = lax.psum_scatter(tuple(grad_sums), ("dp", "seq"), scatter_dimension=0, tiled=True)
    return (
        jnp.stack(outputs),
        jnp.stack(input_grads),
        owned[0],
        owned[1],
        owned[2],
        owned[3],
        owned[4],
        owned[5],
        owned[6],
        owned[7],
        owned[8],
        owned[9],
        owned[10],
        owned[11],
        owned[12],
    )


def solution(mesh):
    placed = (
        P(None, "dp", "seq", None),
        P(None, "dp", "seq"),
        P(None, "dp"),
        P(None, "dp", "seq", None),
        P(("dp", "seq")),
        P(("dp", "seq")),
        P(("dp", "seq"), None),
        P(("dp", "seq")),
        P(("dp", "seq")),
        P(("dp", "seq"), None),
        P(("dp", "seq")),
        P(("dp", "seq")),
        P(("dp", "seq")),
        P(("dp", "seq"), None),
        P(("dp", "seq")),
        P(("dp", "seq"), None),
        P(("dp", "seq")),
    )
    return jax.shard_map(
        on_device,
        mesh=mesh,
        in_specs=placed,
        out_specs=(
            P(None, "dp", "seq", None),
            P(None, "dp", "seq", None),
            P(("dp", "seq")),
            P(("dp", "seq")),
            P(("dp", "seq"), None),
            P(("dp", "seq")),
            P(("dp", "seq")),
            P(("dp", "seq"), None),
            P(("dp", "seq")),
            P(("dp", "seq")),
            P(("dp", "seq")),
            P(("dp", "seq"), None),
            P(("dp", "seq")),
            P(("dp", "seq"), None),
            P(("dp", "seq")),
        ),
        check_vma=False,
    )
```

profile of v0, /device:TPU:0, one launch (start us, length us, event | category | flops | bytes accessed | tf_op | source)
XLA Modules:
  0.0 1872.0 jit_solution(16271196453125605584)
XLA Ops:
  14.7 42.6 %all-reduce.18 = (bf16[1024]{0:T(1024)(128)(2,1)S(1)}, bf16[1024]{0:T(1024)(128)(2,1)S(1)}, bf16[1024]{0:T(1024)(128)(2,1)S(1)}, bf16[1024]{0:T(1024)(128)(2,1)S...) all-reduce(bf16[1024]{0:T(1024)(128)(2,1)S(1)} %dynamic-update-slic, ...), channel_id=1, replica_groups=mesh['dp'=8,'seq'=4] {'dp','seq'}, use_global_device_ids=true, to_apply=%add.1 | all-reduce | flops 8192 | bytes 32768
  64.0 19.3 %all-gather.12.cloned.1.call-done = bf16[1024,3072]{1,0:T(8,128)(2,1)} async-done(((bf16[32,3072]{1,0:T(8,128)(2,1)}), bf16[1024,3072]{1,0:T(8,128)(2,1)}) %all-gather.12.cloned.1.call-update) | async-done | bytes 6291472 | tf_op jit(solution)/shard_map/all_gather | solution.py:48
  105.9 66.4 %all-gather.2 = bf16[32,1,128]{2,1,0:T(2,128)(2,1)S(1)} all-gather(bf16[1,1,128]{2,1,0:T(2,128)(2,1)S(1)} %bitcast.220), channel_id=1, replica_groups=mesh['dp'=8,'seq'=4] {'dp','seq'}, dimensions={0}, use_global_device_ids=true | all-gather | bytes 8448 | tf_op jit(solution)/shard_map/all_gather | solution.py:56
  172.7 16.6 all-gather
  189.4 16.9 all-gather.1
  239.1 19.5 %all-gather.26.cloned.1.call-done = bf16[2,608,1024]{2,1,0:T(8,128)(2,1)} async-done(((bf16[2,152,1024]{2,1,0:T(8,128)(2,1)}), bf16[2,608,1024]{2,1,0:T(8,128)(2,1)}) %all-gather.26.cloned.1.call-update) | async-done | bytes 2490384 | tf_op jit(solution)/shard_map/all_gather | solution.py:148
  261.8 50.3 %all-gather.24.cloned.1.call-done = bf16[2,608,1024]{2,1,0:T(8,128)(2,1)} async-done(((bf16[2,152,1024]{2,1,0:T(8,128)(2,1)}), bf16[2,608,1024]{2,1,0:T(8,128)(2,1)}) %all-gather.24.cloned.1.call-update) | async-done | bytes 2490384 | tf_op jit(solution)/shard_map/all_gather | solution.py:149
  316.6 53.6 %all-gather.18.cloned.1.call-done = bf16[1024,1024]{1,0:T(8,128)(2,1)} async-done(((bf16[32,1024]{1,0:T(8,128)(2,1)}), bf16[1024,1024]{1,0:T(8,128)(2,1)}) %all-gather.18.cloned.1.call-update) | async-done | bytes 2097168 | tf_op jit(solution)/shard_map/all_gather | solution.py:51
  385.6 63.8 %all-gather.20.cloned.1.call-done = bf16[1024,4096]{1,0:T(8,128)(2,1)} async-done(((bf16[32,4096]{1,0:T(8,128)(2,1)}), bf16[1024,4096]{1,0:T(8,128)(2,1)}) %all-gather.20.cloned.1.call-update) | async-done | bytes 8388624 | tf_op jit(solution)/shard_map/all_gather | solution.py:55
  457.5 70.8 %all-gather.22.cloned.1.call-done = bf16[4096,1024]{1,0:T(8,128)(2,1)} async-done(((bf16[128,1024]{1,0:T(8,128)(2,1)}), bf16[4096,1024]{1,0:T(8,128)(2,1)}) %all-gather.22.cloned.1.call-update) | async-done | bytes 8388624 | tf_op jit(solution)/shard_map/all_gather | solution.py:57
  528.4 18.2 convert_reduce_fusion.1
  586.1 11.7 multiply_reduce_fusion.1
  637.3 18.6 convert_reduce_fusion
  664.0 16.1 reduce-scatter.25.cloned.1.call-done
  721.6 12.0 multiply_reduce_fusion
  778.4 44.7 %reduce-scatter.29.cloned.1.call-done = bf16[152,2048]{1,0:T(8,128)(2,1)} async-done(((bf16[608,2048]{1,0:T(8,128)(2,1)}), bf16[152,2048]{1,0:T(8,128)(2,1)}) %reduce-scatter.29.cloned.1.call-update) | async-done | bytes 622608
  826.4 9.4 convolution_add_fusion.2
  843.3 12.8 convolution_add_fusion.1
  869.7 10.4 convolution_add_fusion
  904.6 42.1 %all-reduce.17 = (f32[1024]{0:T(1024)S(1)}, f32[1024]{0:T(1024)S(1)}, f32[1024]{0:T(1024)S(1)}, f32[1024]{0:T(1024)S(1)}, f32[1024]{0:T(1024)S(1)}, /*index=5*/f...) all-reduce(f32[1024]{0:T(1024)S(1)} %add.301, ...), channel_id=8, replica_groups=mesh['dp'=8,'seq'=4] {'dp','seq'}, use_global_device_ids=true, to_apply=%region_28.29.clone | all-reduce | flops 12288 | bytes 98304
  959.7 13.8 reduce-scatter.19.cloned.1.call-done
  973.5 160.2 %reduce-scatter.17.cloned.1.call-done = f32[32,3072]{1,0:T(8,128)} async-done(((f32[1024,3072]{1,0:T(8,128)}), f32[32,3072]{1,0:T(8,128)}) %reduce-scatter.17.cloned.1.call-update) | async-done | bytes 393232 | tf_op jit(solution)/shard_map/reduce_scatter | solution.py:288
  1133.7 366.1 %reduce-scatter.21.cloned.1.call-done = f32[32,4096]{1,0:T(8,128)} async-done(((f32[1024,4096]{1,0:T(8,128)}), f32[32,4096]{1,0:T(8,128)}) %reduce-scatter.21.cloned.1.call-update) | async-done | bytes 524304 | tf_op jit(solution)/shard_map/reduce_scatter | solution.py:288
  1499.9 365.0 %reduce-scatter.23.cloned.1.call-done = f32[128,1024]{1,0:T(8,128)} async-done(((f32[4096,1024]{1,0:T(8,128)}), f32[128,1024]{1,0:T(8,128)}) %reduce-scatter.23.cloned.1.call-update) | async-done | bytes 524304 | tf_op jit(solution)/shard_map/reduce_scatter | solution.py:288
  (448 shorter events, 334.8 us)
Async XLA Ops:
  7.2 76.1 %all-gather.12.cloned.1.call-start = ((), (), s32[]{:S(2)}) async-start(), calls=%async_computation.8 | async-start | bytes 6488064 | tf_op jit(solution)/shard_map/all_gather | solution.py:48
  7.9 205.0 %all-gather.16.cloned.1.call-start = ((), (), s32[]{:S(2)}) async-start(), calls=%async_computation.10 | async-start | bytes 3112960 | tf_op jit(solution)/shard_map/all_gather | solution.py:148
  90.9 125.3 %all-gather.14.cloned.1.call-start = ((), (), s32[]{:S(2)}) async-start(), calls=%async_computation.9 | async-start | bytes 3112960 | tf_op jit(solution)/shard_map/all_gather | solution.py:149
  98.4 108.1 %copy-start.12 = (bf16[2,2,152,1024]{3,2,1,0:T(8,128)(2,1)S(1)}, bf16[2,2,152,1024]{3,2,1,0:T(8,128)(2,1)}, u32[]{:S(2)}) copy-start(bf16[2,2,152,1024]{3,2,1,0:T(8,128)(2,1)} %param.20) | copy-start | bytes 3735556
  98.4 160.2 %all-gather.26.cloned.1.call-start = ((), (), s32[]{:S(2)}) async-start(), calls=%async_computation.15 | async-start | bytes 3112960 | tf_op jit(solution)/shard_map/all_gather | solution.py:148
  100.8 211.3 %all-gather.24.cloned.1.call-start = ((), (), s32[]{:S(2)}) async-start(), calls=%async_computation.14 | async-start | bytes 3112960 | tf_op jit(solution)/shard_map/all_gather | solution.py:149
  101.4 268.9 %all-gather.18.cloned.1.call-start = ((), (), s32[]{:S(2)}) async-start(), calls=%async_computation.11 | async-start | bytes 2162688 | tf_op jit(solution)/shard_map/all_gather | solution.py:51
  101.9 347.5 %all-gather.20.cloned.1.call-start = ((), (), s32[]{:S(2)}) async-start(), calls=%async_computation.12 | async-start | bytes 8650752 | tf_op jit(solution)/shard_map/all_gather | solution.py:55
  102.7 425.7 %all-gather.22.cloned.1.call-start = ((), (), s32[]{:S(2)}) async-start(), calls=%async_computation.13 | async-start | bytes 8650752 | tf_op jit(solution)/shard_map/all_gather | solution.py:57
  103.4 557.2 %reduce-scatter.27.cloned.1.call-start = ((), (), s32[]{:S(2)}) async-start(), calls=%async_computation.21 | async-start | bytes 3112960
  206.4 173.5 %copy-start.66 = (pred[2,608]{1,0:T(4,128)(4,1)}, pred[2,608]{1,0:T(4,128)(4,1)S(1)}, u32[]{:S(2)}) copy-start(pred[2,608]{1,0:T(4,128)(4,1)S(1)} %compare_bitcast_fusion) | copy-start | bytes 3652
  239.1 131.1 %copy-start.38 = (bf16[304,1024]{1,0:T(8,128)(2,1)}, bf16[304,1024]{1,0:T(8,128)(2,1)S(1)}, u32[]{:S(2)}) copy-start(bf16[304,1024]{1,0:T(8,128)(2,1)S(1)} %convert_element_type.337) | copy-start | bytes 1867780
  261.8 112.5 %copy-start.5 = (bf16[2,608,1024]{1,2,0:T(8,128)(2,1)}, bf16[2,608,1024]{1,2,0:T(8,128)(2,1)S(1)}, u32[]{:S(2)}) copy-start(bf16[2,608,1024]{1,2,0:T(8,128)(2,1)S(1)} %copy.129) | copy-start | bytes 7471108
  373.2 177.0 %copy-start.68 = (f32[304]{0:T(512)}, f32[304]{0:T(512)S(1)}, u32[]{:S(2)}) copy-start(f32[304]{0:T(512)S(1)} %broadcast_multiply_fusion.1) | copy-start | bytes 3652
  374.2 175.9 %copy-start.72 = (f32[304]{0:T(512)}, f32[304]{0:T(512)S(1)}, u32[]{:S(2)}) copy-start(f32[304]{0:T(512)S(1)} %fusion.39) | copy-start | bytes 3652
  381.3 68.2 %copy-start.21 = (f32[304,1024]{1,0:T(8,128)S(1)}, f32[304,1024]{1,0:T(8,128)}, u32[]{:S(2)}) copy-start(f32[304,1024]{1,0:T(8,128)} %copy-done.20) | copy-start | bytes 3735556
  449.4 78.9 %copy-start.48 = (bf16[304,1024]{1,0:T(8,128)(2,1)S(1)}, bf16[304,1024]{1,0:T(8,128)(2,1)}, u32[]{:S(2)}) copy-start(bf16[304,1024]{1,0:T(8,128)(2,1)} %fusion.32) | copy-start | bytes 1867780
  570.2 109.9 %reduce-scatter.25.cloned.1.call-start = ((), (), s32[]{:S(2)}) async-start(), calls=%async_computation.20 | async-start | bytes 3112960
  631.2 144.7 %reduce-scatter.31.cloned.1.call-start = ((), (), s32[]{:S(2)}) async-start(), calls=%async_computation.23 | async-start | bytes 3112960
  721.5 101.7 %reduce-scatter.29.cloned.1.call-start = ((), (), s32[]{:S(2)}) async-start(), calls=%async_computation.22 | async-start | bytes 3112960
  751.3 222.3 %reduce-scatter.19.cloned.1.call-start = ((), (), s32[]{:S(2)}) async-start(), calls=%async_computation.17 | async-start | bytes 4325376 | tf_op jit(solution)/shard_map/reduce_scatter | solution.py:288
  756.1 377.6 %reduce-scatter.17.cloned.1.call-start = ((), (), s32[]{:S(2)}) async-start(), calls=%async_computation.16 | async-start | bytes 12976128 | tf_op jit(solution)/shard_map/reduce_scatter | solution.py:288
  835.9 664.0 %reduce-scatter.21.cloned.1.call-start = ((), (), s32[]{:S(2)}) async-start(), calls=%async_computation.18 | async-start | bytes 17301504 | tf_op jit(solution)/shard_map/reduce_scatter | solution.py:288
  856.2 1008.7 %reduce-scatter.23.cloned.1.call-start = ((), (), s32[]{:S(2)}) async-start(), calls=%async_computation.19 | async-start | bytes 17301504 | tf_op jit(solution)/shard_map/reduce_scatter | solution.py:288
  (105 other events, 1019.1 us)
Sparse Core Ops, SparseCore 0:
  10.9 72.3 all-gather.11
  91.1 51.2 all-gather.15
  144.6 60.9 all-gather.13
  206.9 51.6 all-gather.25
  260.6 51.4 all-gather.23
  314.9 55.2 all-gather.17
  373.2 76.2 all-gather.19
  452.4 75.9 all-gather.21
  570.3 48.6 reduce-scatter.26
  631.3 48.7 reduce-scatter.24
  721.6 49.6 reduce-scatter.30
  773.5 49.6 reduce-scatter.28
  826.0 147.4 reduce-scatter.18
  980.0 153.7 reduce-scatter.16
  1136.6 363.2 reduce-scatter.20
  1502.7 362.1 reduce-scatter.22
where the time goes:
time: 1880 us; the launch traced here: 1870 us
  waiting for transfers between devices  1250 us (66%)
  matrix products  225 us (12%)
  blocking collectives  185 us (10%)
  local copies, waits for them, and re-layouts  132 us (7%)
  other arithmetic  66.7 us (4%)
    reduce_scatter x4, waiting for transfers between devices, on_device(): lax.psum_scatter(tuple(grad_sums), ('dp', 'seq'), scatter_dimension=0, ti...  905 us
    unnamed x2, blocking collectives  84.7 us
    unnamed x267, local copies, waits for them, and re-layouts  79.7 us
    all_gather x1, waiting for transfers between devices, fetch_weights(): lax.all_gather(shards[11], ('dp', 'seq'), axis=0, tiled=True)  70.8 us
    all_gather x1, blocking collectives, fetch_weights(): lax.all_gather(shards[10], ('dp', 'seq'), axis=0, tiled=True)  66.4 us
    unnamed x20, waiting for transfers between devices  64.1 us
    all_gather x1, waiting for transfers between devices, fetch_weights(): lax.all_gather(shards[9], ('dp', 'seq'), axis=0, tiled=True)  63.8 us
    dot_general x8, matrix products, matmul_nt(): lax.dot_general(left_side, right_side, (((1,), (1,)), ((), ())), preferre...  59.2 us
  transfers between devices with their start and end apart: 16, of which 12 were waited for; matrix products, arithmetic and copies ran while one was open for 17% of the time, Pallas kernels for 0%

commit v1 on v0

v1 whole, which is shorter than its diff:
```python
import jax
import jax.numpy as jnp
from jax import lax
from jax.sharding import PartitionSpec as P

HEADS = 16


EPSILON = 1e-06
MASKED = -1e30
BOTH = ("dp", "seq")
BF16 = jnp.bfloat16
F32 = jnp.float32


def norm_stats(values):
    center = values - jnp.mean(values, -1, keepdims=True)
    spread = jnp.mean(center * center, -1, keepdims=True)
    inverse = lax.rsqrt(spread + EPSILON)
    return center * inverse, inverse


def norm_back(grads, gain_vec, unit, inverse):
    scaled = grads * gain_vec
    first = jnp.mean(scaled, -1, keepdims=True)
    second = jnp.mean(scaled * unit, -1, keepdims=True)
    return inverse * (scaled - first - unit * second)


def matmul(left_side, right_side):
    return jnp.dot(left_side, right_side, preferred_element_type=F32)


def matmul_tn(left_side, right_side):
    return lax.dot_general(
        left_side, right_side, (((0,), (0,)), ((), ())), preferred_element_type=F32
    )


def matmul_nt(left_side, right_side):
    return lax.dot_general(
        left_side, right_side, (((1,), (1,)), ((), ())), preferred_element_type=F32
    )


def gather(shard):
    return lax.all_gather(shard, BOTH, axis=0, tiled=True)


def scatter(total):
    return lax.psum_scatter(total.astype(BF16), BOTH, scatter_dimension=0, tiled=True).astype(F32)


def gather_vectors(vectors):
    packed = lax.all_gather(jnp.concatenate(vectors), BOTH, axis=0, tiled=False)
    unpacked = []
    start = 0
    for member in vectors:
        extent = member.shape[0]
        unpacked.append(packed[:, start : start + extent].reshape(-1).astype(F32))
        start += extent
    return unpacked


def scatter_vectors(totals, group_size):
    packed = jnp.concatenate([total.reshape(group_size, -1) for total in totals], 1)
    owned = lax.psum_scatter(packed, BOTH, scatter_dimension=0, tiled=True).reshape(-1)
    pieces = []
    start = 0
    for total in totals:
        extent = total.shape[0] // group_size
        pieces.append(owned[start : start + extent])
        start += extent
    return pieces


def exchange(blocks):
    return lax.all_to_all(blocks, "seq", split_axis=0, concat_axis=0, tiled=True)


def to_images(values):
    seq_size = lax.axis_size("seq")
    tail = values.shape[2:]
    swapped = exchange(values.reshape((-1,) + tail))
    by_source = jnp.swapaxes(swapped.reshape((seq_size, -1) + tail), 0, 1)
    return by_source.reshape((by_source.shape[0], seq_size * tail[0]) + tail[1:])


def to_tokens(values, like):
    seq_size = lax.axis_size("seq")
    tail = like.shape[2:]
    by_target = jnp.swapaxes(values.reshape((-1, seq_size) + tail), 0, 1)
    return exchange(by_target.reshape((-1,) + tail)).reshape(like.shape)


def attention_forward(queries, keys, values, okay):
    images, extent, width = queries.shape
    split = (images, extent, HEADS, width // HEADS)
    scores = jnp.einsum(
        "sqhd,skhd->shqk", queries.reshape(split), keys.reshape(split), preferred_element_type=F32
    )
    scores = jnp.where(okay[:, None, None, :] > 0, scores, MASKED)
    exp_scores = jnp.exp(scores - jnp.max(scores, -1, keepdims=True))
    probs = (exp_scores / jnp.sum(exp_scores, -1, keepdims=True)).astype(BF16)
    attended = jnp.einsum("shqk,skhd->sqhd", probs, values.reshape(split), preferred_element_type=F32)
    return attended.reshape(images, extent, width).astype(BF16), probs


def attention_backward(queries, keys, values, probs, grads):
    images, extent, width = queries.shape
    split = (images, extent, HEADS, width // HEADS)
    grad_heads = grads.reshape(split)
    grad_probs = jnp.einsum(
        "sqhd,skhd->shqk", grad_heads, values.reshape(split), preferred_element_type=F32
    )
    exact = probs.astype(F32)
    inner = jnp.sum(exact * grad_probs, -1, keepdims=True)
    grad_scores = (exact * (grad_probs - inner)).astype(BF16)
    scale = (width // HEADS) ** (-0.5)
    gq = jnp.einsum("shqk,skhd->sqhd", grad_scores, keys.reshape(split), preferred_element_type=F32)
    gk = jnp.einsum("shqk,sqhd->skhd", grad_scores, queries.reshape(split), preferred_element_type=F32)
    gv = jnp.einsum("shqk,sqhd->skhd", probs, grad_heads, preferred_element_type=F32)
    shape = (images * extent, width)
    return (
        (gq.astype(BF16) * scale).reshape(shape),
        gk.astype(BF16).reshape(shape),
        gv.astype(BF16).reshape(shape),
    )


def on_device(
    tokens,
    pad_mask,
    image_counts,
    cotangent,
    gain_one,
    shift_one,
    qkv_weight,
    query_bias,
    value_bias,
    out_weight,
    out_bias,
    gain_two,
    shift_two,
    up_weight,
    up_bias,
    down_weight,
    down_bias,
):
    micro_count, slot_count, local_len, width = tokens.shape
    seq_size = lax.axis_size("seq")
    group_size = lax.axis_size(BOTH)
    images = micro_count * slot_count // seq_size
    extent = local_len * seq_size
    rows = images * extent
    query_scale = (width // HEADS) ** (-0.5)

    vectors = gather_vectors(
        [
            gain_one,
            shift_one,
            query_bias,
            value_bias,
            out_bias,
            gain_two,
            shift_two,
            up_bias,
            down_bias,
        ]
    )
    gain1, shift1, qbias, vbias, obias, gain2, shift2, ubias, dbias = vectors
    mix_full = gather(qkv_weight)
    proj_full = gather(out_weight)
    up_full = gather(up_weight)
    down_full = gather(down_weight)

    image_okay = to_images(pad_mask)
    image_rows = to_images(tokens)
    image_grad = to_images(cotangent)

    place = lax.axis_index("seq") * images + jnp.arange(images)
    counts = image_counts[place // slot_count, 0]
    live = (image_okay > 0) & ((place % slot_count) < counts)[:, None]

    x = image_rows.reshape(rows, width).astype(F32)
    unit1, inverse1 = norm_stats(x)
    h1 = (unit1 * gain1 + shift1).astype(BF16)
    mixed = matmul(h1, mix_full)
    queries = ((mixed[:, :width] + qbias) * query_scale).astype(BF16)
    keys = mixed[:, width : 2 * width].astype(BF16)
    values = (mixed[:, 2 * width :] + vbias).astype(BF16)
    per_image = (images, extent, width)
    queries, keys, values = (
        queries.reshape(per_image),
        keys.reshape(per_image),
        values.reshape(per_image),
    )
    attended, probs = attention_forward(queries, keys, values, image_okay)
    attended = attended.reshape(rows, width)
    middle = x + (matmul(attended, proj_full) + obias)
    unit2, inverse2 = norm_stats(middle)
    h2 = (unit2 * gain2 + shift2).astype(BF16)
    pre_act = matmul(h2, up_full) + ubias
    hidden = jax.nn.gelu(pre_act, approximate=False).astype(BF16)
    result = (middle + (matmul(hidden, down_full) + dbias)).astype(BF16)
    block_out = to_tokens(result.reshape(per_image), tokens)

    c = jnp.where(live[..., None], image_grad, jnp.zeros_like(image_grad)).reshape(rows, width)
    w_down, c = lax.optimization_barrier((matmul_tn(hidden, c).astype(BF16), c))
    d_down = scatter(w_down)
    d_dbias = jnp.sum(c.astype(F32), 0)
    gelu_slope = jax.vjp(lambda u: jax.nn.gelu(u, approximate=False), pre_act)[1]
    du = gelu_slope(matmul_nt(c, down_full))[0].astype(BF16)
    w_up, du = lax.optimization_barrier((matmul_tn(h2, du).astype(BF16), du))
    d_up = scatter(w_up)
    d_ubias = jnp.sum(du.astype(F32), 0)
    g2 = matmul_nt(du, up_full)
    d_gain2 = jnp.sum(g2 * unit2, 0)
    d_shift2 = jnp.sum(g2, 0)
    gx2 = c.astype(F32) + norm_back(g2, gain2, unit2, inverse2)
    ga = gx2.astype(BF16)
    w_out, ga = lax.optimization_barrier((matmul_tn(attended, ga).astype(BF16), ga))
    d_out = scatter(w_out)
    d_obias = jnp.sum(ga.astype(F32), 0)
    go = matmul_nt(ga, proj_full).astype(BF16).reshape(per_image)
    gq, gk, gv = attention_backward(queries, keys, values, probs, go)
    gz = jnp.concatenate([gq, gk, gv], 1)
    w_mix, gz = lax.optimization_barrier((matmul_tn(h1, gz).astype(BF16), gz))
    d_mix = scatter(w_mix)
    d_qbias = jnp.sum(gq.astype(F32), 0)
    d_vbias = jnp.sum(gv.astype(F32), 0)
    g1 = matmul_nt(gz, mix_full)
    d_gain1 = jnp.sum(g1 * unit1, 0)
    d_shift1 = jnp.sum(g1, 0)
    gx = gx2 + norm_back(g1, gain1, unit1, inverse1)
    grad_tokens = to_tokens(gx.astype(BF16).reshape(per_image), tokens).astype(F32)
    small = scatter_vectors(
        [
            d_gain1,
            d_shift1,
            d_qbias,
            d_vbias,
            d_obias,
            d_gain2,
            d_shift2,
            d_ubias,
            d_dbias,
        ],
        group_size,
    )
    return (
        block_out,
        grad_tokens,
        small[0],
        small[1],
        d_mix,
        small[2],
        small[3],
        d_out,
        small[4],
        small[5],
        small[6],
        d_up,
        small[7],
        d_down,
        small[8],
    )


def solution(mesh):
    image_spec = P(None, "dp", "seq", None)
    vector = P(BOTH)
    matrix = P(BOTH, None)
    params = (
        vector,
        vector,
        matrix,
        vector,
        vector,
        matrix,
        vector,
        vector,
        vector,
        matrix,
        vector,
        matrix,
        vector,
    )
    return jax.shard_map(
        on_device,
        mesh=mesh,
        in_specs=(image_spec, P(None, "dp", "seq"), P(None, "dp"), image_spec) + params,
        out_specs=(image_spec, image_spec) + params,
        check_vma=False,
    )
```

time: 1880 us -> 1060 us (0.56)
  waiting for transfers between devices: 1250 us -> 548 us
  local copies, waits for them, and re-layouts: 132 us -> 24.6 us
  matrix products: 225 us -> 186 us
  blocking collectives: 185 us -> 205 us
    reduce_scatter x4, waiting for transfers between devices: 905 us -> 465 us  [scatter(): lax.psum_scatter(total.astype(BF16), BOTH, scatter_dimension=0, tiled=True)]
    all_gather x8 -> x4, waiting for transfers between devices: 277 us -> 51.4 us  [gather(): return lax.all_gather(shard, BOTH, axis=0, tiled=True)]
    unnamed x267 -> x79, local copies, waits for them, and re-layouts: 79.7 us -> 10.3 us
    unnamed x20 -> x8, waiting for transfers between devices: 64.1 us -> 4 us
    all_to_all x0 -> x2, blocking collectives: none -> 55.7 us  [exchange(): lax.all_to_all(blocks, 'seq', split_axis=0, concat_axis=0, tiled=True)]
    unnamed x2 -> x1, blocking collectives: 84.7 us -> 49.4 us
    all_to_all x0 -> x3, waiting for transfers between devices: none -> 27.7 us  [exchange(): lax.all_to_all(blocks, 'seq', split_axis=0, concat_axis=0, tiled=True)]
    dot_general x8 -> x4, matrix products: 56.2 us -> 34.5 us  [matmul_tn(): lax.dot_general(left_side, right_side, (((0,), (0,)), ((), ())), preferre...]
  transfers between devices with their start and end apart: 16 -> 11, of which waited for: 12 -> 6; matrix products, arithmetic and copies ran while one was open for 17% -> 18% of each run, Pallas kernels for 0% -> 0%
where the time goes in v1:
time: 1060 us; the launch traced here: 1050 us
  waiting for transfers between devices  548 us (52%)
  blocking collectives  205 us (19%)
  matrix products  186 us (18%)
  other arithmetic  64.4 us (6%)
  local copies, waits for them, and re-layouts  24.6 us (2%)
  between operations  15.6 us (1%)
  starting transfers between devices  11.1 us (1%)
    reduce_scatter x4, waiting for transfers between devices, scatter(): lax.psum_scatter(total.astype(BF16), BOTH, scatter_dimension=0, tiled=True)  465 us
    all_gather x1, blocking collectives, gather_vectors(): packed = lax.all_gather(jnp.concatenate(vectors), BOTH, axis=0, tiled=False)  100 us
    all_to_all x2, blocking collectives, exchange(): lax.all_to_all(blocks, 'seq', split_axis=0, concat_axis=0, tiled=True)  55.7 us
    dot_general x4, matrix products, matmul(): return jnp.dot(left_side, right_side, preferred_element_type=F32)  53 us
    all_gather x4, waiting for transfers between devices, gather(): return lax.all_gather(shard, BOTH, axis=0, tiled=True)  51.4 us
    unnamed x1, blocking collectives  49.4 us
    dot_general x4, matrix products, matmul_nt(): lax.dot_general(left_side, right_side, (((1,), (1,)), ((), ())), preferre...  40.4 us
    dot_general x4, matrix products, matmul_tn(): lax.dot_general(left_side, right_side, (((0,), (0,)), ((), ())), preferre...  34.5 us
  transfers between devices with their start and end apart: 11, of which 6 were waited for; matrix products, arithmetic and copies ran while one was open for 18% of the time, Pallas kernels for 0%

profile of v1, /device:TPU:0, one launch (start us, length us, event | category | flops | bytes accessed | tf_op | source)
XLA Modules:
  0.0 1055.0 jit_solution(17665558730368657325)
XLA Ops:
  10.1 11.7 %all_to_all.29 = s32[4,1,152]{2,1,0:T(1,128)S(1)} all-to-all(s32[4,1,152]{2,1,0:T(1,128)S(1)} %all_to_all.19), channel_id=1, replica_groups=mesh['dp'=8,'seq'=4] {'seq'}, dimensions={0} | all-to-all | bytes 4864 | tf_op jit(solution)/shard_map/all_to_all | solution.py:78
  21.9 44.0 %all_to_all.30 = bf16[4,152,1024]{2,1,0:T(8,128)(2,1)S(1)} all-to-all(bf16[4,152,1024]{2,1,0:T(8,128)(2,1)} %bitcast.126), channel_id=1, replica_groups=mesh['dp'=8,'seq'=4] {'seq'}, dimensions={0} | all-to-all | bytes 2490368 | tf_op jit(solution)/shard_map/all_to_all | solution.py:78
  70.3 100.0 %all-gather.1 = bf16[32,1,384]{2,1,0:T(2,128)(2,1)S(1)} all-gather(bf16[1,1,384]{2,1,0:T(2,128)(2,1)S(1)} %reshape.404), channel_id=2, replica_groups=mesh['dp'=8,'seq'=4] {'dp','seq'}, dimensions={0}, use_global_device_ids=true | all-gather | bytes 25344 | tf_op jit(solution)/shard_map/all_gather | solution.py:55
  192.4 14.5 %fusion.25 = (f32[16,608]{1,0:T(8,128)S(1)}, f32[16,608,608]{1,2,0:T(8,128)}) fusion(pred[608]{0:T(1024)(128)(4,1)S(1)} %gt.24, bf16[608,16,64]{0,2,1:T(8,128)(2,1)} %bitcast.116, bf16[608,16,64]{0,2,1:T(8,128)(2,1)} %bitcast.112), kind=kOutput, calls=%fused_computation.103 | convolution fusion | flops 774816320 | bytes 26188384 | tf_op jit(solution)/shard_map/sub | solution.py:103
  206.9 9.4 divide_convert_fusion
  229.6 16.2 %all-gather.11.cloned.1.call-done = bf16[1024,4096]{1,0:T(8,128)(2,1)} async-done(((bf16[32,4096]{1,0:T(8,128)(2,1)}), bf16[1024,4096]{1,0:T(8,128)(2,1)}) %all-gather.11.cloned.1.call-update) | async-done | bytes 8388624 | tf_op jit(solution)/shard_map/all_gather | solution.py:47
  245.8 32.1 %multiply_convert_fusion = (bf16[608,4096]{1,0:T(8,128)(2,1)S(1)}, f32[608,4096]{1,0:T(8,128)}, f32[608,4096]{1,0:T(8,128)}) fusion(f32[4096]{0:T(1024)S(1)} %fusion.20, bf16[1024,4096]{1,0:T(8,128)(2,1)} %all-gather.11.cloned.1.call-done, f32[608,1024]{1,0:T(8,128)} %copy-done.6, f32[1024]{0:T(1024)S(1)} %reshape.398, f32[1024]{0:T(1024)S(1)} %reshape.397, ...), kind=kOutput, calls=%fused_computation.15 | convolution fusion | flops 5267750912 | bytes 35812096 | tf_op jit(solution)/shard_map/dot_general | solution.py:31
  280.2 9.2 convolution_convert_fusion.1
  289.4 35.2 %all-gather.13.cloned.1.call-done = bf16[4096,1024]{1,0:T(8,128)(2,1)} async-done(((bf16[128,1024]{1,0:T(8,128)(2,1)}), bf16[4096,1024]{1,0:T(8,128)(2,1)}) %all-gather.13.cloned.1.call-update) | async-done | bytes 8388624 | tf_op jit(solution)/shard_map/all_gather | solution.py:47
  324.6 17.0 %add_convert_fusion = bf16[608,4096]{1,0:T(8,128)(2,1)} fusion(f32[608,4096]{1,0:T(8,128)} %get-tuple-element.53, f32[608,4096]{1,0:T(8,128)} %get-tuple-element.77, f32[4096]{0:T(1024)S(1)} %fusion.20, bf16[608,1024]{1,0:T(8,128)(2,1)S(1)} %copy-done.14, bf16[4096,1024]{1,0:T(8,128)(2,1)} %all-gather.13.cloned.1.call-done), kind=kOutput, calls=%fused_computation.14 | convolution fusion | flops 5137629184 | bytes 34553856 | tf_op jit(solution)/shard_map/dot_general | solution.py:41
  341.6 11.8 %convolution_convert_fusion = bf16[1024,4096]{1,0:T(8,128)(2,1)} fusion(bf16[608,4096]{1,0:T(8,128)(2,1)} %add_convert_fusion, f32[608,1024]{1,0:T(8,128)S(1)} %copy-done.7, f32[1024]{0:T(1024)S(1)} %reshape.398, f32[1024]{0:T(1024)S(1)} %reshape.397, f32[608]{0:T(1024)S(1)} %add_rsqrt_fusion, f32[608]{0:T(1024)S(1)} %broadcast_multiply_fusion.4), kind=kOutput, calls=%fused_computation.29 | convolution fusion | flops 5107580928 | bytes 15872768 | tf_op jit(solution)/shard_map/dot_general | solution.py:35
  353.4 10.5 multiply_reduce_fusion
  376.0 16.7 %fusion.1 = (f32[16,608]{1,0:T(8,128)S(1)}, f32[16,608,608]{1,2,0:T(8,128)}) fusion(bf16[16,608,608]{1,2,0:T(8,128)(2,1)} %copy-done.2, bf16[608,16,64]{0,2,1:T(8,128)(2,1)} %bitcast.110, bf16[608,16,64]{0,2,1:T(8,128)(2,1)S(1)} %bitcast.109), kind=kOutput, calls=%fused_computation.3 | convolution fusion | flops 774806016 | bytes 38017024 | tf_op jit(solution)/shard_map/sqhd,skhd->shqk/dot_general | solution.py:113
  392.8 21.5 %fusion.2 = bf16[16,608,608]{1,2,0:T(8,128)(2,1)} fusion(f32[16,608,608]{1,2,0:T(8,128)} %get-tuple-element.80, f32[16,608]{1,0:T(8,128)S(1)} %get-tuple-element.79, f32[16,608,608]{1,2,0:T(8,128)} %get-tuple-element.74, f32[16,608]{1,0:T(8,128)S(1)} %copy-done.20), kind=kLoop, calls=%fused_computation.4 | loop fusion | flops 35487744 | bytes 59224064 | tf_op jit(solution)/shard_map/convert_element_type | solution.py:118
  414.3 8.5 convert_reduce_fusion.2
  438.2 9.6 pad_maximum_fusion
  447.8 10.4 convolution_convert_fusion.2
  460.7 10.5 add_convert_fusion.2
  475.0 8.8 multiply_reduce_fusion.1
  485.8 27.7 %all-to-all-done.2 = bf16[4,152,1024]{2,1,0:T(8,128)(2,1)S(1)} async-done(((bf16[4,152,1024]{2,1,0:T(8,128)(2,1)}), bf16[4,152,1024]{2,1,0:T(8,128)(2,1)S(1)}, u32[]{:S(2)}, u32[]{:S(2)}) %all-to-all-start.2) | async-done | bytes 1245216 | tf_op jit(solution)/shard_map/all_to_all | solution.py:78
  522.7 49.4 %all-reduce = f32[32,384]{1,0:T(8,128)S(1)} all-reduce(f32[32,384]{1,0:T(8,128)S(1)} %concatenate.15), channel_id=3, replica_groups=mesh['dp'=8,'seq'=4] {'dp','seq'}, use_global_device_ids=true, to_apply=%region_20.21.clone | all-reduce | flops 12288 | bytes 98304
  576.5 95.3 %reduce-scatter.5.cloned.1.call-done = bf16[32,3072]{1,0:T(8,128)(2,1)} async-done(((bf16[1024,3072]{1,0:T(8,128)(2,1)}), bf16[32,3072]{1,0:T(8,128)(2,1)}) %reduce-scatter.5.cloned.1.call-update) | async-done | bytes 196624 | tf_op jit(solution)/shard_map/reduce_scatter | solution.py:51
  673.6 185.7 %reduce-scatter.9.cloned.1.call-done = bf16[32,4096]{1,0:T(8,128)(2,1)} async-done(((bf16[1024,4096]{1,0:T(8,128)(2,1)}), bf16[32,4096]{1,0:T(8,128)(2,1)}) %reduce-scatter.9.cloned.1.call-update) | async-done | bytes 262160 | tf_op jit(solution)/shard_map/reduce_scatter | solution.py:51
  861.0 184.0 %reduce-scatter.11.cloned.1.call-done = bf16[128,1024]{1,0:T(8,128)(2,1)} async-done(((bf16[4096,1024]{1,0:T(8,128)(2,1)}), bf16[128,1024]{1,0:T(8,128)(2,1)}) %reduce-scatter.11.cloned.1.call-update) | async-done | bytes 262160 | tf_op jit(solution)/shard_map/reduce_scatter | solution.py:51
  (166 shorter events, 99.8 us)
Async XLA Ops:
  7.2 164.2 %copy-start = (s32[2,1]{0,1:T(1,128)S(1)}, s32[2,1]{0,1:T(1,128)}, u32[]{:S(2)}) copy-start(s32[2,1]{0,1:T(1,128)} %param.19) | copy-start | bytes 28
  7.2 168.4 %all-gather.7.cloned.1.call-start = ((), (), s32[]{:S(2)}) async-start(), calls=%async_computation.9 | async-start | bytes 6488064 | tf_op jit(solution)/shard_map/all_gather | solution.py:47
  7.9 216.1 %all-gather.9.cloned.1.call-start = ((), (), s32[]{:S(2)}) async-start(), calls=%async_computation.10 | async-start | bytes 2162688 | tf_op jit(solution)/shard_map/all_gather | solution.py:47
  8.7 237.1 %all-gather.11.cloned.1.call-start = ((), (), s32[]{:S(2)}) async-start(), calls=%async_computation.11 | async-start | bytes 8650752 | tf_op jit(solution)/shard_map/all_gather | solution.py:47
  21.8 48.3 %copy-start.28 = (bf16[32]{0:T(256)(128)(2,1)S(1)}, bf16[32]{0:T(256)(128)(2,1)}, u32[]{:S(2)}) copy-start(bf16[32]{0:T(256)(128)(2,1)} %param.21) | copy-start | bytes 196
  21.8 48.3 %copy-start.29 = (bf16[32]{0:T(256)(128)(2,1)S(1)}, bf16[32]{0:T(256)(128)(2,1)}, u32[]{:S(2)}) copy-start(bf16[32]{0:T(256)(128)(2,1)} %param.22) | copy-start | bytes 196
  21.8 48.3 %copy-start.30 = (bf16[32]{0:T(256)(128)(2,1)S(1)}, bf16[32]{0:T(256)(128)(2,1)}, u32[]{:S(2)}) copy-start(bf16[32]{0:T(256)(128)(2,1)} %param.24) | copy-start | bytes 196
  21.8 48.3 %copy-start.31 = (bf16[32]{0:T(256)(128)(2,1)S(1)}, bf16[32]{0:T(256)(128)(2,1)}, u32[]{:S(2)}) copy-start(bf16[32]{0:T(256)(128)(2,1)} %param.25) | copy-start | bytes 196
  21.8 48.3 %copy-start.32 = (bf16[32]{0:T(256)(128)(2,1)S(1)}, bf16[32]{0:T(256)(128)(2,1)}, u32[]{:S(2)}) copy-start(bf16[32]{0:T(256)(128)(2,1)} %param.27) | copy-start | bytes 196
  21.8 48.3 %copy-start.33 = (bf16[32]{0:T(256)(128)(2,1)S(1)}, bf16[32]{0:T(256)(128)(2,1)}, u32[]{:S(2)}) copy-start(bf16[32]{0:T(256)(128)(2,1)} %param.28) | copy-start | bytes 196
  21.8 48.3 %copy-start.34 = (bf16[32]{0:T(256)(128)(2,1)S(1)}, bf16[32]{0:T(256)(128)(2,1)}, u32[]{:S(2)}) copy-start(bf16[32]{0:T(256)(128)(2,1)} %param.29) | copy-start | bytes 196
  21.8 48.3 %copy-start.35 = (bf16[128]{0:T(256)(128)(2,1)S(1)}, bf16[128]{0:T(256)(128)(2,1)}, u32[]{:S(2)}) copy-start(bf16[128]{0:T(256)(128)(2,1)} %param.31) | copy-start | bytes 772
  21.9 48.3 %copy-start.36 = (bf16[32]{0:T(256)(128)(2,1)S(1)}, bf16[32]{0:T(256)(128)(2,1)}, u32[]{:S(2)}) copy-start(bf16[32]{0:T(256)(128)(2,1)} %param.33) | copy-start | bytes 196
  65.9 158.2 %copy-start.3 = (bf16[4,152,1024]{2,1,0:T(8,128)(2,1)}, bf16[4,152,1024]{2,1,0:T(8,128)(2,1)S(1)}, u32[]{:S(2)}) copy-start(bf16[4,152,1024]{2,1,0:T(8,128)(2,1)S(1)} %all_to_all.30) | copy-start | bytes 3735556
  65.9 107.9 %all-to-all-start.3 = ((bf16[4,152,1024]{2,1,0:T(8,128)(2,1)}), bf16[4,152,1024]{2,1,0:T(8,128)(2,1)S(1)}, u32[]{:S(2)}, u32[]{:S(2)}) async-start(bf16[4,152,1024]{2,1,0:T(8,128)(2,1)} %bitcast.127), calls=%async_computation.3 | async-start | bytes 2490368 | tf_op jit(solution)/shard_map/all_to_all | solution.py:78
  69.4 255.1 %all-gather.13.cloned.1.call-start = ((), (), s32[]{:S(2)}) async-start(), calls=%async_computation.12 | async-start | bytes 8650752 | tf_op jit(solution)/shard_map/all_gather | solution.py:47
  70.0 505.0 %reduce-scatter.7.cloned.1.call-start = ((), (), s32[]{:S(2)}) async-start(), calls=%async_computation.14 | async-start | bytes 2162688 | tf_op jit(solution)/shard_map/reduce_scatter | solution.py:51
  229.6 50.6 %copy-start.14 = (bf16[608,1024]{1,0:T(8,128)(2,1)S(1)}, bf16[608,1024]{1,0:T(8,128)(2,1)}, u32[]{:S(2)}) copy-start(bf16[608,1024]{1,0:T(8,128)(2,1)} %bitcast_select_fusion) | copy-start | bytes 3735556
  392.7 279.1 %reduce-scatter.5.cloned.1.call-start = ((), (), s32[]{:S(2)}) async-start(), calls=%async_computation.13 | async-start | bytes 6488064 | tf_op jit(solution)/shard_map/reduce_scatter | solution.py:51
  458.2 401.0 %reduce-scatter.9.cloned.1.call-start = ((), (), s32[]{:S(2)}) async-start(), calls=%async_computation.15 | async-start | bytes 8650752 | tf_op jit(solution)/shard_map/reduce_scatter | solution.py:51
  459.0 586.0 %reduce-scatter.11.cloned.1.call-start = ((), (), s32[]{:S(2)}) async-start(), calls=%async_computation.16 | async-start | bytes 8650752 | tf_op jit(solution)/shard_map/reduce_scatter | solution.py:51
  471.3 42.2 %all-to-all-start.2 = ((bf16[4,152,1024]{2,1,0:T(8,128)(2,1)}), bf16[4,152,1024]{2,1,0:T(8,128)(2,1)S(1)}, u32[]{:S(2)}, u32[]{:S(2)}) async-start(bf16[4,152,1024]{2,1,0:T(8,128)(2,1)} %bitcast.128), calls=%async_computation.2 | async-start | bytes 2490368 | tf_op jit(solution)/shard_map/all_to_all | solution.py:78
  513.4 59.9 %all-to-all-start.4 = ((bf16[4,152,1024]{2,1,0:T(8,128)(2,1)}), bf16[4,152,1024]{2,1,0:T(8,128)(2,1)S(1)}, u32[]{:S(2)}, u32[]{:S(2)}) async-start(bf16[4,152,1024]{2,1,0:T(8,128)(2,1)} %bitcast.29), calls=%async_computation.4 | async-start | bytes 2490368 | tf_op jit(solution)/shard_map/all_to_all | solution.py:78
  573.3 474.6 %copy-start.1 = (s32[2,1]{0,1:T(1,128)S(1)}, s32[2,1]{0,1:T(1,128)}, u32[]{:S(2)}) copy-start(s32[2,1]{0,1:T(1,128)} %param.19) | copy-start | bytes 28
  (25 other events, 167.3 us)
Sparse Core Ops, SparseCore 0:
  10.9 90.4 all-gather.6
  104.4 62.1 all-gather.8
  169.5 76.2 all-gather.10
  248.6 75.9 all-gather.12
  392.8 149.1 reduce-scatter.6
  548.5 123.3 reduce-scatter.4
  674.1 185.0 reduce-scatter.8
  861.5 183.4 reduce-scatter.10

commit v2 on v1

--- a/solution.py
+++ b/solution.py
@@ -1,6 +1,8 @@
 import jax
 import jax.numpy as jnp
 from jax import lax
+from jax.experimental import pallas as pl
+from jax.experimental.pallas import tpu as pltpu
 from jax.sharding import PartitionSpec as P
 
 HEADS = 16
@@ -43,16 +45,72 @@
     )
 
 
-def gather(shard):
-    return lax.all_gather(shard, BOTH, axis=0, tiled=True)
-
-
-def scatter(total):
-    return lax.psum_scatter(total.astype(BF16), BOTH, scatter_dimension=0, tiled=True).astype(F32)
+def stage_list(swap):
+    dp_bits = lax.axis_size("dp").bit_length() - 1
+    seq_bits = lax.axis_size("seq").bit_length() - 1
+    rest = list(range(1, dp_bits))
+    if swap:
+        rest.reverse()
+    order = [("dp", bit) for bit in [0] + rest]
+    return order + [("seq", bit) for bit in range(seq_bits)], dp_bits, seq_bits
+
+
+def stage_place(stage, dp_bits, seq_bits):
+    axis, bit = stage
+    return dp_bits - 1 - bit if axis == "dp" else dp_bits + seq_bits - 1 - bit
+
+
+def my_bit(stage):
+    axis, bit = stage
+    return (lax.axis_index(axis) >> bit) & 1
+
+
+def swap_halves(block, stage):
+    axis, bit = stage
+    pairs = [(i, i ^ (1 << bit)) for i in range(lax.axis_size(axis))]
+    return lax.ppermute(block, axis, pairs)
+
+
+def gather(shard, swap=False):
+    stages, dp_bits, seq_bits = stage_list(swap)
+    depth = dp_bits + seq_bits
+    whole = (2,) * depth + shard.shape
+    starts = [None] * depth
+    for stage in stages:
+        starts[stage_place(stage, dp_bits, seq_bits)] = my_bit(stage)
+    starts += [0] * shard.ndim
+    sizes = [1] * depth + list(shard.shape)
+    buffer = jnp.zeros(whole, shard.dtype)
+    block = shard.reshape(sizes)
+    buffer = lax.dynamic_update_slice(buffer, block, starts)
+    for index, stage in enumerate(reversed(stages)):
+        place = stage_place(stage, dp_bits, seq_bits)
+        if index > 0:
+            block = lax.dynamic_slice(buffer, starts, sizes)
+        other = list(starts)
+        other[place] = 1 - starts[place]
+        buffer = lax.dynamic_update_slice(buffer, swap_halves(block, stage), other)
+        starts[place] = 0
+        sizes[place] = 2
+    return buffer.reshape((-1,) + shard.shape[1:])
+
+
+def scatter(total, swap=False):
+    stages, dp_bits, seq_bits = stage_list(swap)
+    depth = dp_bits + seq_bits
+    block = total.reshape((2,) * depth + (total.shape[0] >> depth,) + total.shape[1:])
+    for stage in stages:
+        place = stage_place(stage, dp_bits, seq_bits)
+        mine = my_bit(stage)
+        sent = lax.dynamic_slice_in_dim(block, 1 - mine, 1, place)
+        kept = lax.dynamic_slice_in_dim(block, mine, 1, place)
+        got = swap_halves(sent, stage)
+        block = (kept.astype(F32) + got.astype(F32)).astype(total.dtype)
+    return block.reshape((-1,) + total.shape[1:]).astype(F32)
 
 
 def gather_vectors(vectors):
-    packed = lax.all_gather(jnp.concatenate(vectors), BOTH, axis=0, tiled=False)
+    packed = gather(jnp.concatenate(vectors)[None])
     unpacked = []
     start = 0
     for member in vectors:
@@ -64,7 +122,7 @@
 
 def scatter_vectors(totals, group_size):
     packed = jnp.concatenate([total.reshape(group_size, -1) for total in totals], 1)
-    owned = lax.psum_scatter(packed, BOTH, scatter_dimension=0, tiled=True).reshape(-1)
+    owned = scatter(packed).reshape(-1)
     pieces = []
     start = 0
     for total in totals:
@@ -75,7 +133,18 @@
 
 
 def exchange(blocks):
-    return lax.all_to_all(blocks, "seq", split_axis=0, concat_axis=0, tiled=True)
+    size = lax.axis_size("seq")
+    me = lax.axis_index("seq")
+    groups = blocks.reshape((size, -1) + blocks.shape[1:])
+    own = lax.dynamic_index_in_dim(groups, me, 0)
+    out = lax.dynamic_update_index_in_dim(jnp.zeros_like(groups), own, me, 0)
+    for shift in range(1, size):
+        target = lax.rem(me + shift, size)
+        source = lax.rem(me + size - shift, size)
+        pairs = [(i, (i + shift) % size) for i in range(size)]
+        got = lax.ppermute(lax.dynamic_index_in_dim(groups, target, 0), "seq", pairs)
+        out = lax.dynamic_update_index_in_dim(out, got, source, 0)
+    return out.reshape(blocks.shape)
 
 
 def to_images(values):
@@ -93,39 +162,103 @@
     return exchange(by_target.reshape((-1,) + tail)).reshape(like.shape)
 
 
-def attention_forward(queries, keys, values, okay):
-    images, extent, width = queries.shape
-    split = (images, extent, HEADS, width // HEADS)
-    scores = jnp.einsum(
-        "sqhd,skhd->shqk", queries.reshape(split), keys.reshape(split), preferred_element_type=F32
-    )
-    scores = jnp.where(okay[:, None, None, :] > 0, scores, MASKED)
-    exp_scores = jnp.exp(scores - jnp.max(scores, -1, keepdims=True))
-    probs = (exp_scores / jnp.sum(exp_scores, -1, keepdims=True)).astype(BF16)
-    attended = jnp.einsum("shqk,skhd->sqhd", probs, values.reshape(split), preferred_element_type=F32)
-    return attended.reshape(images, extent, width).astype(BF16), probs
-
-
-def attention_backward(queries, keys, values, probs, grads):
-    images, extent, width = queries.shape
-    split = (images, extent, HEADS, width // HEADS)
-    grad_heads = grads.reshape(split)
-    grad_probs = jnp.einsum(
-        "sqhd,skhd->shqk", grad_heads, values.reshape(split), preferred_element_type=F32
-    )
-    exact = probs.astype(F32)
-    inner = jnp.sum(exact * grad_probs, -1, keepdims=True)
-    grad_scores = (exact * (grad_probs - inner)).astype(BF16)
-    scale = (width // HEADS) ** (-0.5)
-    gq = jnp.einsum("shqk,skhd->sqhd", grad_scores, keys.reshape(split), preferred_element_type=F32)
-    gk = jnp.einsum("shqk,sqhd->skhd", grad_scores, queries.reshape(split), preferred_element_type=F32)
-    gv = jnp.einsum("shqk,sqhd->skhd", probs, grad_heads, preferred_element_type=F32)
+def forward_kernel(okay_ref, q_ref, k_ref, v_ref, out_ref, prob_ref):
+    okay = okay_ref[0] > 0
+    head = q_ref.shape[2] // 2
+    parts = []
+    for j in range(2):
+        lanes = slice(j * head, (j + 1) * head)
+        scores = matmul_nt(k_ref[0, :, lanes], q_ref[0, :, lanes])
+        scores = jnp.where(okay, scores, MASKED)
+        exp_scores = jnp.exp(scores - jnp.max(scores, 0, keepdims=True))
+        scale = 1.0 / jnp.sum(exp_scores, 0, keepdims=True)
+        probs = (exp_scores * scale).astype(BF16)
+        prob_ref[0, j] = probs
+        parts.append(matmul_tn(v_ref[0, :, lanes], probs))
+    out_ref[0] = jnp.concatenate(parts, 0).T.astype(BF16)
+
+
+def backward_kernel(q_ref, k_ref, v_ref, prob_ref, go_ref, gq_ref, gk_ref, gv_ref):
+    head = q_ref.shape[2] // 2
+    scale = head ** (-0.5)
+    parts = []
+    for j in range(2):
+        lanes = slice(j * head, (j + 1) * head)
+        go = go_ref[0, :, lanes]
+        probs = prob_ref[0, j]
+        exact = probs.astype(F32)
+        grad_probs = matmul_nt(v_ref[0, :, lanes], go)
+        inner = jnp.sum(exact * grad_probs, 0, keepdims=True)
+        grad_scores = (exact * (grad_probs - inner)).astype(BF16)
+        parts.append(matmul_tn(k_ref[0, :, lanes], grad_scores))
+        gk_ref[0, :, lanes] = matmul(grad_scores, q_ref[0, :, lanes]).astype(BF16)
+        gv_ref[0, :, lanes] = matmul(probs, go).astype(BF16)
+    gq_ref[0] = (jnp.concatenate(parts, 0).T.astype(BF16) * scale).astype(BF16)
+
+
+def column_spec(extent, lanes, offset):
+    return pl.BlockSpec((1, extent, lanes), lambda i, h: (i, 0, h + offset))
+
+
+def attention_forward(mixed, okay):
+    images, extent, triple = mixed.shape
+    width = triple // 3
+    lanes = 2 * width // HEADS
+    pairs = HEADS // 2
+    elements = images * HEADS * extent * extent
+    return pl.pallas_call(
+        forward_kernel,
+        grid=(images, pairs),
+        in_specs=[
+            pl.BlockSpec((1, extent, 1), lambda i, h: (i, 0, 0)),
+            column_spec(extent, lanes, 0),
+            column_spec(extent, lanes, pairs),
+            column_spec(extent, lanes, 2 * pairs),
+        ],
+        out_specs=[
+            column_spec(extent, lanes, 0),
+            pl.BlockSpec((1, 2, extent, extent), lambda i, h: (i, h, 0, 0)),
+        ],
+        out_shape=[
+            jax.ShapeDtypeStruct((images, extent, width), BF16),
+            jax.ShapeDtypeStruct((images, HEADS, extent, extent), BF16),
+        ],
+        compiler_params=pltpu.CompilerParams(vmem_limit_bytes=40 * 1024 * 1024),
+        cost_estimate=pl.CostEstimate(
+            flops=4 * elements * lanes // 2,
+            bytes_accessed=2 * elements + 8 * images * extent * width,
+            transcendentals=elements,
+        ),
+    )(okay[..., None].astype(F32), mixed, mixed, mixed)
+
+
+def attention_backward(mixed, probs, grads):
+    images, extent, triple = mixed.shape
+    width = triple // 3
+    lanes = 2 * width // HEADS
+    pairs = HEADS // 2
+    elements = images * HEADS * extent * extent
+    gq, gk, gv = pl.pallas_call(
+        backward_kernel,
+        grid=(images, pairs),
+        in_specs=[
+            column_spec(extent, lanes, 0),
+            column_spec(extent, lanes, pairs),
+            column_spec(extent, lanes, 2 * pairs),
+            pl.BlockSpec((1, 2, extent, extent), lambda i, h: (i, h, 0, 0)),
+            column_spec(extent, lanes, 0),
+        ],
+        out_specs=[column_spec(extent, lanes, 0)] * 3,
+        out_shape=[jax.ShapeDtypeStruct((images, extent, width), BF16)] * 3,
+        compiler_params=pltpu.CompilerParams(vmem_limit_bytes=40 * 1024 * 1024),
+        cost_estimate=pl.CostEstimate(
+            flops=8 * elements * lanes // 2,
+            bytes_accessed=2 * elements + 14 * images * extent * width,
+            transcendentals=0,
+        ),
+    )(mixed, mixed, mixed, probs, grads)
     shape = (images * extent, width)
-    return (
-        (gq.astype(BF16) * scale).reshape(shape),
-        gk.astype(BF16).reshape(shape),
-        gv.astype(BF16).reshape(shape),
-    )
+    return gq.reshape(shape), gk.reshape(shape), gv.reshape(shape)
 
 
 def on_device(
@@ -170,8 +303,8 @@
     )
     gain1, shift1, qbias, vbias, obias, gain2, shift2, ubias, dbias = vectors
     mix_full = gather(qkv_weight)
-    proj_full = gather(out_weight)
-    up_full = gather(up_weight)
+    proj_full = gather(out_weight, True)
+    up_full = gather(up_weight, True)
     down_full = gather(down_weight)
 
     image_okay = to_images(pad_mask)
@@ -185,17 +318,12 @@
     x = image_rows.reshape(rows, width).astype(F32)
     unit1, inverse1 = norm_stats(x)
     h1 = (unit1 * gain1 + shift1).astype(BF16)
-    mixed = matmul(h1, mix_full)
-    queries = ((mixed[:, :width] + qbias) * query_scale).astype(BF16)
-    keys = mixed[:, width : 2 * width].astype(BF16)
-    values = (mixed[:, 2 * width :] + vbias).astype(BF16)
+    mixed_bias = jnp.concatenate([qbias, jnp.zeros_like(qbias), vbias])
+    mixed_scale = jnp.where(jnp.arange(3 * width) < width, query_scale, 1.0)
+    mixed = ((matmul(h1, mix_full) + mixed_bias) * mixed_scale).astype(BF16)
     per_image = (images, extent, width)
-    queries, keys, values = (
-        queries.reshape(per_image),
-        keys.reshape(per_image),
-        values.reshape(per_image),
-    )
-    attended, probs = attention_forward(queries, keys, values, image_okay)
+    mixed = mixed.reshape(images, extent, 3 * width)
+    attended, probs = attention_forward(mixed, image_okay)
     attended = attended.reshape(rows, width)
     middle = x + (matmul(attended, proj_full) + obias)
     unit2, inverse2 = norm_stats(middle)
@@ -212,7 +340,7 @@
     gelu_slope = jax.vjp(lambda u: jax.nn.gelu(u, approximate=False), pre_act)[1]
     du = gelu_slope(matmul_nt(c, down_full))[0].astype(BF16)
     w_up, du = lax.optimization_barrier((matmul_tn(h2, du).astype(BF16), du))
-    d_up = scatter(w_up)
+    d_up = scatter(w_up, True)
     d_ubias = jnp.sum(du.astype(F32), 0)
     g2 = matmul_nt(du, up_full)
     d_gain2 = jnp.sum(g2 * unit2, 0)
@@ -223,10 +351,11 @@
     d_out = scatter(w_out)
     d_obias = jnp.sum(ga.astype(F32), 0)
     go = matmul_nt(ga, proj_full).astype(BF16).reshape(per_image)
-    gq, gk, gv = attention_backward(queries, keys, values, probs, go)
+    gq, gk, gv = attention_backward(mixed, probs, go)
     gz = jnp.concatenate([gq, gk, gv], 1)
     w_mix, gz = lax.optimization_barrier((matmul_tn(h1, gz).astype(BF16), gz))
-    d_mix = scatter(w_mix)
+    near = 3 * width // 2
+    d_mix = jnp.concatenate([scatter(w_mix[:, :near]), scatter(w_mix[:, near:], True)], 1)
     d_qbias = jnp.sum(gq.astype(F32), 0)
     d_vbias = jnp.sum(gv.astype(F32), 0)
     g1 = matmul_nt(gz, mix_full)

time: 1060 us -> 732 us (0.69)
  waiting for transfers between devices: 548 us -> 314 us
  blocking collectives: 205 us -> 0 us
  local copies, waits for them, and re-layouts: 24.6 us -> 128 us
  starting transfers between devices: 11.1 us -> 88.3 us
  matrix products: 186 us -> 119 us
  Pallas kernels: 0 us -> 40.6 us
  other arithmetic: 64.4 us -> 31.3 us
  between operations: 15.6 us -> 3.06 us
    reduce_scatter x4 -> x0, waiting for transfers between devices: 465 us -> none  [scatter(): lax.psum_scatter(total.astype(BF16), BOTH, scatter_dimension=0, tiled=True)]
    ppermute x0 -> x70, waiting for transfers between devices: none -> 314 us  [the longest x55 288 us: swap_halves(): return lax.ppermute(block, axis, pairs)]
    all_gather x1 -> x0, blocking collectives: 100 us -> none  [gather_vectors(): packed = lax.all_gather(jnp.concatenate(vectors), BOTH, axis=0, tiled=False)]
    ppermute x0 -> x70, starting transfers between devices: none -> 88.3 us  [the longest x55 57.7 us: swap_halves(): return lax.ppermute(block, axis, pairs)]
    all_to_all x2 -> x0, blocking collectives: 55.7 us -> none  [exchange(): lax.all_to_all(blocks, 'seq', split_axis=0, concat_axis=0, tiled=True)]
    all_gather x4 -> x0, waiting for transfers between devices: 51.4 us -> none  [gather(): return lax.all_gather(shard, BOTH, axis=0, tiled=True)]
    unnamed x1 -> x0, blocking collectives: 49.4 us -> none
    dynamic_slice x0 -> x55, local copies, waits for them, and re-layouts: none -> 48.1 us  [the longest x20 31.3 us: gather(): block = lax.dynamic_slice(buffer, starts, sizes)]
  transfers between devices with their start and end apart: 11 -> 70, of which waited for: 6 -> 31; matrix products, arithmetic and copies ran while one was open for 18% -> 28% of each run, Pallas kernels for 0% -> 6%
where the time goes in v2:
time: 732 us; the launch traced here: 724 us
  waiting for transfers between devices  314 us (43%)
  local copies, waits for them, and re-layouts  128 us (17%)
  matrix products  119 us (16%)
  starting transfers between devices  88.3 us (12%)
  Pallas kernels  40.6 us (6%)
  other arithmetic  31.3 us (4%)
    ppermute x55, waiting for transfers between devices, swap_halves(): return lax.ppermute(block, axis, pairs)  288 us
    ppermute x55, starting transfers between devices, swap_halves(): return lax.ppermute(block, axis, pairs)  57.7 us
    dot_general x4, matrix products, matmul(): return jnp.dot(left_side, right_side, preferred_element_type=F32)  48.3 us
    dot_general x4, matrix products, matmul_nt(): lax.dot_general(left_side, right_side, (((1,), (1,)), ((), ())), preferre...  38.3 us
    dynamic_update_slice x25, local copies, waits for them, and re-layouts, gather(): buffer = lax.dynamic_update_slice(buffer, swap_halves(block, stage), other)  32.6 us
    dot_general x4, matrix products, matmul_tn(): lax.dot_general(left_side, right_side, (((0,), (0,)), ((), ())), preferre...  32.3 us
    dynamic_slice x20, local copies, waits for them, and re-layouts, gather(): block = lax.dynamic_slice(buffer, starts, sizes)  31.3 us
    ppermute x15, starting transfers between devices, exchange(): lax.ppermute(lax.dynamic_index_in_dim(groups, target, 0), 'seq', pairs)  30.6 us
  transfers between devices with their start and end apart: 70, of which 31 were waited for; matrix products, arithmetic and copies ran while one was open for 28% of the time, Pallas kernels for 6%

profile of v2, /device:TPU:0, one launch (start us, length us, event | category | flops | bytes accessed | tf_op | source)
XLA Modules:
  0.0 723.9 jit_solution(18335489791744827619)
XLA Ops:
  61.5 16.8 %collective-permute-done.17 = bf16[1,1,1,2,1,32,1024]{6,5,4,3,2,1,0:T(8,128)(2,1)} collective-permute-done((bf16[1,1,1,2,1,32,1024]{6,5,4,3,2,1,0:T(8,128)(2,1)}, bf16[1,1,1,2,1,32,1024]{6,5,4,3,2,1,0:T(8,128)(2,1)}, u32[]{:S(2)}, u32[]{:S(2)}) %collective-permute-start.17) | collective-permute-done | bytes 131104 | tf_op jit(solution)/shard_map/ppermute | solution.py:71
  84.6 11.4 %collective-permute-start = (bf16[1,1,152,1024]{3,2,0,1:T(8,128)(2,1)}, bf16[1,1,152,1024]{3,2,0,1:T(8,128)(2,1)S(1)}, u32[]{:S(2)}, u32[]{:S(2)}) collective-permute-start(bf16[1,1,152,1024]{3,2,0,1:T(8,128)(2,1)} %get-tuple-element.81), channel_id=1, source_target_pairs={{0,1},{1,2},{2,3},{3,0},{4,5},{5,6},{6,7},{7,4},{8,9},{9,10},{10,1... | collective-permute-start | bytes 933896 | tf_op jit(solution)/shard_map/ppermute | solution.py:145
  121.9 18.9 %collective-permute-done.22 = bf16[1,1,1,2,1,32,4096]{6,5,4,3,2,1,0:T(8,128)(2,1)S(1)} collective-permute-done((bf16[1,1,1,2,1,32,4096]{6,5,4,3,2,1,0:T(8,128)(2,1)S(1)}, bf16[1,1,1,2,1,32,4096]{6,5,4,3,2,1,0:T(8,128)(2,1)S(1)}, u32[]{:S(2)}, u32[]{:S(2)}) %collective-permute-start.22) | collective-permute-done | bytes 524320 | tf_op jit(solution)/shard_map/ppermute | solution.py:71
  147.8 21.2 %collective-permute-done.23 = bf16[1,1,1,2,2,32,4096]{6,5,4,3,2,1,0:T(8,128)(2,1)S(1)} collective-permute-done((bf16[1,1,1,2,2,32,4096]{6,5,4,3,2,1,0:T(8,128)(2,1)S(1)}, bf16[1,1,1,2,2,32,4096]{6,5,4,3,2,1,0:T(8,128)(2,1)S(1)}, u32[]{:S(2)}, u32[]{:S(2)}) %collective-permute-start.23) | collective-permute-done | bytes 1048608 | tf_op jit(solution)/shard_map/ppermute | solution.py:71
  182.9 18.8 %collective-permute-done.14 = bf16[2,1,1,2,2,32,3072]{6,5,4,3,2,1,0:T(8,128)(2,1)S(1)} collective-permute-done((bf16[2,1,1,2,2,32,3072]{6,5,4,3,2,1,0:T(8,128)(2,1)S(1)}, bf16[2,1,1,2,2,32,3072]{6,5,4,3,2,1,0:T(8,128)(2,1)S(1)}, u32[]{:S(2)}, u32[]{:S(2)}) %collective-permute-start.14) | collective-permute-done | bytes 1572896 | tf_op jit(solution)/shard_map/ppermute | solution.py:71
  208.1 25.0 %collective-permute-done.19 = bf16[1,2,1,2,2,32,1024]{6,5,4,3,2,1,0:T(8,128)(2,1)S(1)} collective-permute-done((bf16[1,2,1,2,2,32,1024]{6,5,4,3,2,1,0:T(8,128)(2,1)}, bf16[1,2,1,2,2,32,1024]{6,5,4,3,2,1,0:T(8,128)(2,1)S(1)}, u32[]{:S(2)}, u32[]{:S(2)}) %collective-permute-start.19) | collective-permute-done | bytes 524320 | tf_op jit(solution)/shard_map/ppermute | solution.py:71
  235.3 17.6 %collective-permute-done.28 = bf16[1,1,1,2,2,128,1024]{6,5,4,3,2,1,0:T(8,128)(2,1)} collective-permute-done((bf16[1,1,1,2,2,128,1024]{6,5,4,3,2,1,0:T(8,128)(2,1)}, bf16[1,1,1,2,2,128,1024]{6,5,4,3,2,1,0:T(8,128)(2,1)}, u32[]{:S(2)}, u32[]{:S(2)}) %collective-permute-start.28) | collective-permute-done | bytes 1048608 | tf_op jit(solution)/shard_map/ppermute | solution.py:71
  267.1 34.8 %collective-permute-done.29 = bf16[2,1,1,2,2,128,1024]{6,5,4,3,2,1,0:T(8,128)(2,1)S(1)} collective-permute-done((bf16[2,1,1,2,2,128,1024]{6,5,4,3,2,1,0:T(8,128)(2,1)S(1)}, bf16[2,1,1,2,2,128,1024]{6,5,4,3,2,1,0:T(8,128)(2,1)S(1)}, u32[]{:S(2)}, u32[]{:S(2)}) %collective-permute-start.29) | collective-permute-done | bytes 2097184 | tf_op jit(solution)/shard_map/ppermute | solution.py:71
  319.1 17.8 %shard_map.280 = (bf16[1,608,1024]{2,1,0:T(8,128)(2,1)S(1)}, bf16[1,16,608,608]{3,2,1,0:T(8,128)(2,1)}) custom-call(f32[1,608,1]{2,1,0:T(8,128)S(1)} %convert_element_type.557.okay_ref, bf16[1,608,3072]{2,1,0:T(8,128)(2,1)S(1)} %fusion.6.q_ref.k_ref.v_ref, bf16[1,608,3072]{2,1,0:T(8,128)(2,1)S(1)} %fusion.6.q_ref.k_ref.v_ref, ...), custom_call_target="tpu_custom_call" | custom-call | flops 1514143744 | bytes 16809984 | tf_op jit(solution)/shard_map/pallas_call | solution.py:209
  341.6 30.1 %multiply_convert_fusion = (bf16[608,4096]{1,0:T(8,128)(2,1)S(1)}, f32[608,4096]{1,0:T(8,128)}, f32[608,4096]{1,0:T(8,128)}) fusion(f32[4096]{0:T(1024)S(1)} %copy-done.35, bf16[1024,4096]{1,0:T(8,128)(2,1)S(1)} %bitcast.126, f32[608,1024]{1,0:T(8,128)S(1)} %get-tuple-element.104, f32[1024]{0:T(1024)S(1)} %copy-done.38, f32[1024]{0:T(1024)S(1)} %copy-done.28, ...), kind=kOutput, calls=%fused_computation.4 | convolution fusion | flops 5267750912 | bytes 35812096 | tf_op jit(solution)/shard_map/dot_general | solution.py:33
  371.7 9.1 %convolution_convert_fusion.1 = bf16[4096,1024]{1,0:T(8,128)(2,1)} fusion(bf16[608,4096]{1,0:T(8,128)(2,1)S(1)} %get-tuple-element.62, bf16[608,1024]{1,0:T(8,128)(2,1)S(1)} %bitcast_select_fusion), kind=kOutput, calls=%fused_computation.21 | convolution fusion | flops 5104467968 | bytes 14614528 | tf_op jit(solution)/shard_map/dot_general | solution.py:37
  385.7 16.8 %add_convert_fusion = bf16[608,4096]{1,0:T(8,128)(2,1)} fusion(f32[608,4096]{1,0:T(8,128)} %get-tuple-element.63, f32[608,4096]{1,0:T(8,128)} %get-tuple-element.105, f32[4096]{0:T(1024)S(1)} %copy-done.35, bf16[608,1024]{1,0:T(8,128)(2,1)S(1)} %copy-done.16, bf16[4096,1024]{1,0:T(8,128)(2,1)} %bitcast.13), kind=kOutput, calls=%fused_computation.3 | convolution fusion | flops 5137629184 | bytes 34553856 | tf_op jit(solution)/shard_map/dot_general | solution.py:43
  402.5 11.8 %convolution_convert_fusion = bf16[1024,4096]{1,0:T(8,128)(2,1)} fusion(bf16[608,4096]{1,0:T(8,128)(2,1)} %add_convert_fusion, f32[608,1024]{1,0:T(8,128)S(1)} %get-tuple-element.104, f32[1024]{0:T(1024)S(1)} %copy-done.38, f32[1024]{0:T(1024)S(1)} %copy-done.28, f32[608]{0:T(1024)S(1)} %add_rsqrt_fusion, f32[608]{0:T(1024)S(1)} %broadcast_multiply_fusion.4), kind=kOutput, calls=%fused_computation.20 | convolution fusion | flops 5107580928 | bytes 15872768 | tf_op jit(solution)/shard_map/dot_general | solution.py:37
  414.4 8.5 %multiply_reduce_fusion = (f32[1024]{0:T(1024)S(1)}, f32[608]{0:T(1024)S(1)}, f32[608]{0:T(1024)S(1)}, f32[1024]{0:T(1024)S(1)}, f32[608,1024]{1,0:T(8,128)S(1)}) fusion(f32[608,1024]{1,0:T(8,128)S(1)} %get-tuple-element.104, f32[608]{0:T(1024)S(1)} %add_rsqrt_fusion, f32[608]{0:T(1024)S(1)} %broadcast_multiply_fusion.4, f32[1024]{0:T(1024)S(1)} %copy-done.28, ...), kind=kOutput, calls=%fused_computation.32 | convolution fusion | flops 5105873920 | bytes 18372096 | tf_op jit(solution)/shard_map/dot_general | solution.py:43
  451.9 22.8 %shard_map.281 = (bf16[1,608,1024]{2,1,0:T(8,128)(2,1)S(1)}, bf16[1,608,1024]{2,1,0:T(8,128)(2,1)S(1)}, bf16[1,608,1024]{2,1,0:T(8,128)(2,1)S(1)}) custom-call(bf16[1,608,3072]{2,1,0:T(8,128)(2,1)S(1)} %copy-done.3, bf16[1,608,3072]{2,1,0:T(8,128)(2,1)S(1)} %copy-done.3, bf16[1,608,3072]{2,1,0:T(8,128)(2,1)S(1)} %copy-done.3, ...), custom_call_target="tpu_custom_call" | custom-call | flops 3028287488 | bytes 20545536 | tf_op jit(solution)/shard_map/pallas_call | solution.py:241
  482.0 8.1 %convolution_convert_fusion.2 = bf16[1024,3072]{1,0:T(8,128)(2,1)} fusion(f32[1024]{0:T(1024)S(1)} %copy-done.27, f32[1024]{0:T(1024)S(1)} %copy-done.25, f32[608]{0:T(1024)S(1)} %copy-done.29, f32[608]{0:T(1024)S(1)} %copy-done.31, bf16[608,1024]{1,0:T(8,128)(2,1)S(1)} %bitcast.121, bf16[608,1024]{1,0:T(8,128)(2,1)S(1)} %bitcast.123, ...), kind=kOutput, calls=%fused_computation.23 | convolution fusion | flops 3843293184 | bytes 11285248 | tf_op jit(solution)/shard_map/dot_general | solution.py:37
  490.2 8.8 %multiply_reduce_fusion.1 = (f32[1024]{0:T(1024)S(1)}, f32[608]{0:T(1024)S(1)}, f32[608]{0:T(1024)S(1)}, f32[1024]{0:T(1024)S(1)}, f32[608,1024]{1,0:T(8,128)}) fusion(f32[608]{0:T(1024)S(1)} %copy-done.29, f32[608]{0:T(1024)S(1)} %copy-done.31, bf16[4,1,152,1024]{3,2,0,1:T(8,128)(2,1)S(1)} %copy-done.10, f32[1024]{0:T(1024)S(1)} %copy-done.25, ...), kind=kOutput, calls=%fused_computation.36 | convolution fusion | flops 3833295872 | bytes 15029760 | tf_op jit(solution)/shard_map/dot_general | solution.py:43
  539.6 8.8 %collective-permute-done.37 = bf16[1,1,152,1024]{3,2,0,1:T(8,128)(2,1)S(1)} collective-permute-done((bf16[1,1,152,1024]{3,2,0,1:T(8,128)(2,1)S(1)}, bf16[1,1,152,1024]{3,2,0,1:T(8,128)(2,1)S(1)}, u32[]{:S(2)}, u32[]{:S(2)}) %collective-permute-start.37) | collective-permute-done | bytes 311328 | tf_op jit(solution)/shard_map/ppermute | solution.py:145
  583.4 15.4 %collective-permute-done.51 = bf16[1,2,1,2,2,32,1536]{6,5,4,3,2,1,0:T(8,128)(2,1)S(1)} collective-permute-done((bf16[1,2,1,2,2,32,1536]{6,5,4,3,2,1,0:T(8,128)(2,1)S(1)}, bf16[1,2,1,2,2,32,1536]{6,5,4,3,2,1,0:T(8,128)(2,1)S(1)}, u32[]{:S(2)}, u32[]{:S(2)}) %collective-permute-start.51) | collective-permute-done | bytes 786464 | tf_op jit(solution)/shard_map/ppermute | solution.py:71
  622.8 32.6 %collective-permute-done.66 = bf16[2,1,1,2,2,128,1024]{6,5,4,3,2,1,0:T(8,128)(2,1)S(1)} collective-permute-done((bf16[2,1,1,2,2,128,1024]{6,5,4,3,2,1,0:T(8,128)(2,1)S(1)}, bf16[2,1,1,2,2,128,1024]{6,5,4,3,2,1,0:T(8,128)(2,1)S(1)}, u32[]{:S(2)}, u32[]{:S(2)}) %collective-permute-start.66) | collective-permute-done | bytes 2097184 | tf_op jit(solution)/shard_map/ppermute | solution.py:71
  667.1 15.0 %collective-permute-done.67 = bf16[1,1,1,2,2,128,1024]{6,5,4,3,2,1,0:T(8,128)(2,1)S(1)} collective-permute-done((bf16[1,1,1,2,2,128,1024]{6,5,4,3,2,1,0:T(8,128)(2,1)S(1)}, bf16[1,1,1,2,2,128,1024]{6,5,4,3,2,1,0:T(8,128)(2,1)S(1)}, u32[]{:S(2)}, u32[]{:S(2)}) %collective-permute-start.67) | collective-permute-done | bytes 1048608 | tf_op jit(solution)/shard_map/ppermute | solution.py:71
  685.1 15.2 %collective-permute-done.68 = bf16[1,1,1,2,1,128,1024]{6,5,4,3,2,1,0:T(8,128)(2,1)S(1)} collective-permute-done((bf16[1,1,1,2,1,128,1024]{6,5,4,3,2,1,0:T(8,128)(2,1)S(1)}, bf16[1,1,1,2,1,128,1024]{6,5,4,3,2,1,0:T(8,128)(2,1)S(1)}, u32[]{:S(2)}, u32[]{:S(2)}) %collective-permute-start.68) | collective-permute-done | bytes 524320 | tf_op jit(solution)/shard_map/ppermute | solution.py:71
  700.6 8.2 %collective-permute-done.63 = bf16[1,1,1,2,1,32,4096]{6,5,4,3,2,1,0:T(8,128)(2,1)S(1)} collective-permute-done((bf16[1,1,1,2,1,32,4096]{6,5,4,3,2,1,0:T(8,128)(2,1)S(1)}, bf16[1,1,1,2,1,32,4096]{6,5,4,3,2,1,0:T(8,128)(2,1)S(1)}, u32[]{:S(2)}, u32[]{:S(2)}) %collective-permute-start.63) | collective-permute-done | bytes 524320 | tf_op jit(solution)/shard_map/ppermute | solution.py:71
  711.2 7.9 %collective-permute-done.69 = bf16[1,1,1,1,1,128,1024]{6,5,4,3,2,1,0:T(8,128)(2,1)S(1)} collective-permute-done((bf16[1,1,1,1,1,128,1024]{6,5,4,3,2,1,0:T(8,128)(2,1)S(1)}, bf16[1,1,1,1,1,128,1024]{6,5,4,3,2,1,0:T(8,128)(2,1)S(1)}, u32[]{:S(2)}, u32[]{:S(2)}) %collective-permute-start.69) | collective-permute-done | bytes 262176 | tf_op jit(solution)/shard_map/ppermute | solution.py:71
  (428 shorter events, 319.3 us)
Async XLA Ops:
  1.4 46.7 %collective-permute-start.5 = (s32[1,1,152]{2,0,1:T(1,128)S(1)}, s32[1,1,152]{2,0,1:T(1,128)S(1)}, u32[]{:S(2)}, u32[]{:S(2)}) collective-permute-start(s32[1,1,152]{2,0,1:T(1,128)S(1)} %get-tuple-element.91), channel_id=1, source_target_pairs={{0,3},{1,0},{2,1},{3,2},{4,7},{5,4},{6,5},{7,6},{8,11},{9,8},{10,9... | collective-permute-start | bytes 1832 | tf_op jit(solution)/shard_map/ppermute | solution.py:145
  6.5 39.5 %collective-permute-start.4 = (s32[1,1,152]{2,0,1:T(1,128)S(1)}, s32[1,1,152]{2,0,1:T(1,128)S(1)}, u32[]{:S(2)}, u32[]{:S(2)}) collective-permute-start(s32[1,1,152]{2,0,1:T(1,128)S(1)} %get-tuple-element.92), channel_id=1, source_target_pairs={{0,2},{1,3},{2,0},{3,1},{4,6},{5,7},{6,4},{7,5},{8,10},{9,11},{10,... | collective-permute-start | bytes 1832 | tf_op jit(solution)/shard_map/ppermute | solution.py:145
  6.5 38.5 %collective-permute-start.3 = (s32[1,1,152]{2,0,1:T(1,128)S(1)}, s32[1,1,152]{2,0,1:T(1,128)S(1)}, u32[]{:S(2)}, u32[]{:S(2)}) collective-permute-start(s32[1,1,152]{2,0,1:T(1,128)S(1)} %get-tuple-element.93), channel_id=1, source_target_pairs={{0,1},{1,2},{2,3},{3,0},{4,5},{5,6},{6,7},{7,4},{8,9},{9,10},{10,1... | collective-permute-start | bytes 1832 | tf_op jit(solution)/shard_map/ppermute | solution.py:145
  46.0 52.7 %collective-permute-start.26 = (bf16[1,1,1,1,1,128,1024]{6,5,4,3,2,1,0:T(8,128)(2,1)}, bf16[1,1,1,1,1,128,1024]{6,5,4,3,2,1,0:T(8,128)(2,1)}, u32[]{:S(2)}, u32[]{:S(2)}) collective-permute-start(bf16[1,1,1,1,1,128,1024]{6,5,4,3,2,1,0:T(8,128)(2,1)} %bitcast.12), channel_id=1, source_target_pairs={{0,2},{1,3},{2,0},{3,1},{4,6},{5,7},{6,4},{7,5},{8,10},{9,11},{10,... | collective-permute-start | bytes 786440 | tf_op jit(solution)/shard_map/ppermute | solution.py:71
  50.4 213.8 %collective-permute-start.36 = (bf16[1,1,152,1024]{3,2,0,1:T(8,128)(2,1)}, bf16[1,1,152,1024]{3,2,0,1:T(8,128)(2,1)}, u32[]{:S(2)}, u32[]{:S(2)}) collective-permute-start(bf16[1,1,152,1024]{3,2,0,1:T(8,128)(2,1)} %get-tuple-element.71), channel_id=1, source_target_pairs={{0,3},{1,0},{2,1},{3,2},{4,7},{5,4},{6,5},{7,6},{8,11},{9,8},{10,9... | collective-permute-start | bytes 933896 | tf_op jit(solution)/shard_map/ppermute | solution.py:145
  107.2 67.9 %collective-permute-start.18 = (bf16[1,1,1,2,2,32,1024]{6,5,4,3,2,1,0:T(8,128)(2,1)S(1)}, bf16[1,1,1,2,2,32,1024]{6,5,4,3,2,1,0:T(8,128)(2,1)S(1)}, u32[]{:S(2)}, u32[]{:S(2)}) collective-permute-start(bf16[1,1,1,2,2,32,1024]{6,5,4,3,2,1,0:T(8,128)(2,1)S(1)} %constant_dynamic-slice_fusion.54), channel_id=1, source_target_pairs={{0,8},{4,12},{8,0},{12,4},{16,24},{20,28},{24,16},{28,20},{1,9},{5... | collective-permute-start | bytes 786440 | tf_op jit(solution)/shard_map/ppermute | solution.py:71
  109.9 68.3 %collective-permute-start.27 = (bf16[1,1,1,2,1,128,1024]{6,5,4,3,2,1,0:T(8,128)(2,1)S(1)}, bf16[1,1,1,2,1,128,1024]{6,5,4,3,2,1,0:T(8,128)(2,1)S(1)}, u32[]{:S(2)}, u32[]{:S(2)}) collective-permute-start(bf16[1,1,1,2,1,128,1024]{6,5,4,3,2,1,0:T(8,128)(2,1)S(1)} %constant_dynamic-slice_fusion.47), channel_id=1, source_target_pairs={{0,1},{1,0},{2,3},{3,2},{4,5},{5,4},{6,7},{7,6},{8,9},{9,8},{10,11... | collective-permute-start | bytes 1572872 | tf_op jit(solution)/shard_map/ppermute | solution.py:71
  146.1 55.6 %collective-permute-start.14 = (bf16[2,1,1,2,2,32,3072]{6,5,4,3,2,1,0:T(8,128)(2,1)S(1)}, bf16[2,1,1,2,2,32,3072]{6,5,4,3,2,1,0:T(8,128)(2,1)S(1)}, u32[]{:S(2)}, u32[]{:S(2)}) collective-permute-start(bf16[2,1,1,2,2,32,3072]{6,5,4,3,2,1,0:T(8,128)(2,1)S(1)} %constant_dynamic-slice_fusion.57), channel_id=1, source_target_pairs={{0,8},{4,12},{8,0},{12,4},{16,24},{20,28},{24,16},{28,20},{1,9},{5... | collective-permute-start | bytes 4718600 | tf_op jit(solution)/shard_map/ppermute | solution.py:71
  173.1 84.0 %collective-permute-start.24 = (bf16[1,2,1,2,2,32,4096]{6,5,4,3,2,1,0:T(8,128)(2,1)}, bf16[1,2,1,2,2,32,4096]{6,5,4,3,2,1,0:T(8,128)(2,1)}, u32[]{:S(2)}, u32[]{:S(2)}) collective-permute-start(bf16[1,2,1,2,2,32,4096]{6,5,4,3,2,1,0:T(8,128)(2,1)} %constant_dynamic-slice_fusion.49), channel_id=1, source_target_pairs={{0,16},{4,20},{8,24},{12,28},{16,0},{20,4},{24,8},{28,12},{1,17},{... | collective-permute-start | bytes 6291464 | tf_op jit(solution)/shard_map/ppermute | solution.py:71
  177.7 55.4 %collective-permute-start.19 = (bf16[1,2,1,2,2,32,1024]{6,5,4,3,2,1,0:T(8,128)(2,1)}, bf16[1,2,1,2,2,32,1024]{6,5,4,3,2,1,0:T(8,128)(2,1)S(1)}, u32[]{:S(2)}, u32[]{:S(2)}) collective-permute-start(bf16[1,2,1,2,2,32,1024]{6,5,4,3,2,1,0:T(8,128)(2,1)} %constant_dynamic-slice_fusion.53), channel_id=1, source_target_pairs={{0,16},{4,20},{8,24},{12,28},{16,0},{20,4},{24,8},{28,12},{1,17},{... | collective-permute-start | bytes 1572872 | tf_op jit(solution)/shard_map/ppermute | solution.py:71
  181.3 71.5 %collective-permute-start.28 = (bf16[1,1,1,2,2,128,1024]{6,5,4,3,2,1,0:T(8,128)(2,1)}, bf16[1,1,1,2,2,128,1024]{6,5,4,3,2,1,0:T(8,128)(2,1)}, u32[]{:S(2)}, u32[]{:S(2)}) collective-permute-start(bf16[1,1,1,2,2,128,1024]{6,5,4,3,2,1,0:T(8,128)(2,1)} %constant_dynamic-slice_fusion.46), channel_id=1, source_target_pairs={{0,16},{4,20},{8,24},{12,28},{16,0},{20,4},{24,8},{28,12},{1,17},{... | collective-permute-start | bytes 3145736 | tf_op jit(solution)/shard_map/ppermute | solution.py:71
  206.7 101.4 %collective-permute-start.15 = (bf16[2,2,1,2,2,32,3072]{6,5,4,3,2,1,0:T(8,128)(2,1)}, bf16[2,2,1,2,2,32,3072]{6,5,4,3,2,1,0:T(8,128)(2,1)}, u32[]{:S(2)}, u32[]{:S(2)}) collective-permute-start(bf16[2,2,1,2,2,32,3072]{6,5,4,3,2,1,0:T(8,128)(2,1)} %constant_dynamic-slice_fusion.56), channel_id=1, source_target_pairs={{0,4},{4,0},{8,12},{12,8},{16,20},{20,16},{24,28},{28,24},{1,5},{5... | collective-permute-start | bytes 9437192 | tf_op jit(solution)/shard_map/ppermute | solution.py:71
  257.1 44.8 %collective-permute-start.29 = (bf16[2,1,1,2,2,128,1024]{6,5,4,3,2,1,0:T(8,128)(2,1)S(1)}, bf16[2,1,1,2,2,128,1024]{6,5,4,3,2,1,0:T(8,128)(2,1)S(1)}, u32[]{:S(2)}, u32[]{:S(2)}) collective-permute-start(bf16[2,1,1,2,2,128,1024]{6,5,4,3,2,1,0:T(8,128)(2,1)S(1)} %constant_dynamic-slice_fusion.45), channel_id=1, source_target_pairs={{0,8},{4,12},{8,0},{12,4},{16,24},{20,28},{24,16},{28,20},{1,9},{5... | collective-permute-start | bytes 6291464 | tf_op jit(solution)/shard_map/ppermute | solution.py:71
  263.6 77.1 %collective-permute-start.25 = (bf16[2,2,1,2,2,32,4096]{6,5,4,3,2,1,0:T(8,128)(2,1)S(1)}, bf16[2,2,1,2,2,32,4096]{6,5,4,3,2,1,0:T(8,128)(2,1)S(1)}, u32[]{:S(2)}, u32[]{:S(2)}) collective-permute-start(bf16[2,2,1,2,2,32,4096]{6,5,4,3,2,1,0:T(8,128)(2,1)S(1)} %constant_dynamic-slice_fusion.48), channel_id=1, source_target_pairs={{0,4},{4,0},{8,12},{12,8},{16,20},{20,16},{24,28},{28,24},{1,5},{5... | collective-permute-start | bytes 12582920 | tf_op jit(solution)/shard_map/ppermute | solution.py:71
  308.2 72.6 %collective-permute-start.30 = (bf16[2,2,1,2,2,128,1024]{6,5,4,3,2,1,0:T(8,128)(2,1)}, bf16[2,2,1,2,2,128,1024]{6,5,4,3,2,1,0:T(8,128)(2,1)}, u32[]{:S(2)}, u32[]{:S(2)}) collective-permute-start(bf16[2,2,1,2,2,128,1024]{6,5,4,3,2,1,0:T(8,128)(2,1)} %constant_dynamic-slice_fusion.44), channel_id=1, source_target_pairs={{0,4},{4,0},{8,12},{12,8},{16,20},{20,16},{24,28},{28,24},{1,5},{5... | collective-permute-start | bytes 12582920 | tf_op jit(solution)/shard_map/ppermute | solution.py:71
  444.2 91.7 %collective-permute-start.33 = (bf16[1,1,152,1024]{3,2,0,1:T(8,128)(2,1)}, bf16[1,1,152,1024]{3,2,0,1:T(8,128)(2,1)S(1)}, u32[]{:S(2)}, u32[]{:S(2)}) collective-permute-start(bf16[1,1,152,1024]{3,2,0,1:T(8,128)(2,1)} %get-tuple-element.75), channel_id=1, source_target_pairs={{0,3},{1,0},{2,1},{3,2},{4,7},{5,4},{6,5},{7,6},{8,11},{9,8},{10,9... | collective-permute-start | bytes 933896 | tf_op jit(solution)/shard_map/ppermute | solution.py:145
  447.7 86.6 %collective-permute-start.32 = (bf16[1,1,152,1024]{3,2,0,1:T(8,128)(2,1)}, bf16[1,1,152,1024]{3,2,0,1:T(8,128)(2,1)S(1)}, u32[]{:S(2)}, u32[]{:S(2)}) collective-permute-start(bf16[1,1,152,1024]{3,2,0,1:T(8,128)(2,1)} %get-tuple-element.76), channel_id=1, source_target_pairs={{0,2},{1,3},{2,0},{3,1},{4,6},{5,7},{6,4},{7,5},{8,10},{9,11},{10,... | collective-permute-start | bytes 933896 | tf_op jit(solution)/shard_map/ppermute | solution.py:145
  447.7 82.3 %collective-permute-start.31 = (bf16[1,1,152,1024]{3,2,0,1:T(8,128)(2,1)}, bf16[1,1,152,1024]{3,2,0,1:T(8,128)(2,1)S(1)}, u32[]{:S(2)}, u32[]{:S(2)}) collective-permute-start(bf16[1,1,152,1024]{3,2,0,1:T(8,128)(2,1)} %get-tuple-element.77), channel_id=1, source_target_pairs={{0,1},{1,2},{2,3},{3,0},{4,5},{5,6},{6,7},{7,4},{8,9},{9,10},{10,1... | collective-permute-start | bytes 933896 | tf_op jit(solution)/shard_map/ppermute | solution.py:145
  480.7 51.0 %collective-permute-start.55 = (bf16[2,2,1,2,2,32,1024]{6,5,4,3,2,1,0:T(8,128)(2,1)}, bf16[2,2,1,2,2,32,1024]{6,5,4,3,2,1,0:T(8,128)(2,1)}, u32[]{:S(2)}, u32[]{:S(2)}) collective-permute-start(bf16[2,2,1,2,2,32,1024]{6,5,4,3,2,1,0:T(8,128)(2,1)} %constant_dynamic-slice_fusion.12), channel_id=1, source_target_pairs={{0,4},{4,0},{8,12},{12,8},{16,20},{20,16},{24,28},{28,24},{1,5},{5... | collective-permute-start | bytes 3145736 | tf_op jit(solution)/shard_map/ppermute | solution.py:71
  548.4 57.7 %collective-permute-start.65 = (bf16[2,2,1,2,2,128,1024]{6,5,4,3,2,1,0:T(8,128)(2,1)}, bf16[2,2,1,2,2,128,1024]{6,5,4,3,2,1,0:T(8,128)(2,1)}, u32[]{:S(2)}, u32[]{:S(2)}) collective-permute-start(bf16[2,2,1,2,2,128,1024]{6,5,4,3,2,1,0:T(8,128)(2,1)} %constant_dynamic-slice_fusion.2), channel_id=1, source_target_pairs={{0,4},{4,0},{8,12},{12,8},{16,20},{20,16},{24,28},{28,24},{1,5},{5... | collective-permute-start | bytes 12582920 | tf_op jit(solution)/shard_map/ppermute | solution.py:71
  554.5 56.4 %collective-permute-start.60 = (bf16[2,2,1,2,2,32,4096]{6,5,4,3,2,1,0:T(8,128)(2,1)}, bf16[2,2,1,2,2,32,4096]{6,5,4,3,2,1,0:T(8,128)(2,1)}, u32[]{:S(2)}, u32[]{:S(2)}) collective-permute-start(bf16[2,2,1,2,2,32,4096]{6,5,4,3,2,1,0:T(8,128)(2,1)} %constant_dynamic-slice_fusion.7), channel_id=1, source_target_pairs={{0,4},{4,0},{8,12},{12,8},{16,20},{20,16},{24,28},{28,24},{1,5},{5... | collective-permute-start | bytes 12582920 | tf_op jit(solution)/shard_map/ppermute | solution.py:71
  610.1 45.3 %collective-permute-start.66 = (bf16[2,1,1,2,2,128,1024]{6,5,4,3,2,1,0:T(8,128)(2,1)S(1)}, bf16[2,1,1,2,2,128,1024]{6,5,4,3,2,1,0:T(8,128)(2,1)S(1)}, u32[]{:S(2)}, u32[]{:S(2)}) collective-permute-start(bf16[2,1,1,2,2,128,1024]{6,5,4,3,2,1,0:T(8,128)(2,1)S(1)} %constant_dynamic-slice_fusion.1), channel_id=1, source_target_pairs={{0,8},{4,12},{8,0},{12,4},{16,24},{20,28},{24,16},{28,20},{1,9},{5... | collective-permute-start | bytes 6291464 | tf_op jit(solution)/shard_map/ppermute | solution.py:71
  614.6 48.6 %collective-permute-start.61 = (bf16[1,2,1,2,2,32,4096]{6,5,4,3,2,1,0:T(8,128)(2,1)S(1)}, bf16[1,2,1,2,2,32,4096]{6,5,4,3,2,1,0:T(8,128)(2,1)S(1)}, u32[]{:S(2)}, u32[]{:S(2)}) collective-permute-start(bf16[1,2,1,2,2,32,4096]{6,5,4,3,2,1,0:T(8,128)(2,1)S(1)} %constant_dynamic-slice_fusion.6), channel_id=1, source_target_pairs={{0,16},{4,20},{8,24},{12,28},{16,0},{20,4},{24,8},{28,12},{1,17},{... | collective-permute-start | bytes 6291464 | tf_op jit(solution)/shard_map/ppermute | solution.py:71
  618.5 48.5 %collective-permute-start.49 = (bf16[1,1,1,1,1,32,1536]{6,5,4,3,2,1,0:T(8,128)(2,1)S(1)}, bf16[1,1,1,1,1,32,1536]{6,5,4,3,2,1,0:T(8,128)(2,1)S(1)}, u32[]{:S(2)}, u32[]{:S(2)}) collective-permute-start(bf16[1,1,1,1,1,32,1536]{6,5,4,3,2,1,0:T(8,128)(2,1)S(1)} %constant_dynamic-slice_fusion.18), channel_id=1, source_target_pairs={{0,2},{1,3},{2,0},{3,1},{4,6},{5,7},{6,4},{7,5},{8,10},{9,11},{10,... | collective-permute-start | bytes 294920 | tf_op jit(solution)/shard_map/ppermute | solution.py:71
  (94 other events, 1908.5 us)
